TPU v7x, 32 devices: a whole 2x2x4 slice. The times are simulated.
32 devices in a mesh: dp: 8 (over z, y), expert: 4 (over x, core).
Axes of the slice: x: 2, y: 2, z: 4, core: 2. Of those that a mesh axis runs over, the one named last changes fastest.
Arguments:
- tokens: bfloat16 [3, 32, 197, 384], P(None, ('dp', 'expert')), may hold values from -6 to 6
- expert_index: int32 [3, 32, 197, 2], P(None, ('dp', 'expert')), may hold values from 0 to 3, as said below
- expert_slot: int32 [3, 32, 197, 2], P(None, ('dp', 'expert')), may hold values from 0 to 127, as said below
- route_kept: int32 [3, 32, 197, 2], P(None, ('dp', 'expert')), may hold values from 0 to 1, as said below
- ln1_gain: bfloat16 [384], P('dp'), may hold values from 0.5 to 1.5
- w_qkv: bfloat16 [384, 1152], P('dp'), may hold values from -0.3125 to 0.3125
- w_out: bfloat16 [384, 384], P('dp'), may hold values from -1.5 to 1.5
- ln2_gain: bfloat16 [384], P('dp'), may hold values from 0.5 to 1.5
- w_router: bfloat16 [384, 4], P('dp'), may hold values from -0.21875 to 0.21875
- expert_in: bfloat16 [4, 384, 1536], P('expert', 'dp'), may hold values from -0.3125 to 0.3125
- expert_bias: bfloat16 [4, 1536], P('expert', 'dp'), may hold values from -3 to 3
- expert_out: bfloat16 [4, 1536, 384], P('expert', 'dp'), may hold values from -3.5 to 3.5
- cotangent: bfloat16 [3, 32, 197, 384], P(None, ('dp', 'expert')), may hold values from -6 to 6
Outputs:
- output: bfloat16 [3, 32, 197, 384], P(None, ('dp', 'expert'))
- d_tokens: float32 [3, 32, 197, 384], P(None, ('dp', 'expert'))
- d_ln1_gain: float32 [384], P('dp')
- d_w_qkv: float32 [384, 1152], P('dp')
- d_w_out: float32 [384, 384], P('dp')
- d_ln2_gain: float32 [384], P('dp')
- d_w_router: float32 [384, 4], P('dp')
- d_expert_in: float32 [4, 384, 1536], P('expert', 'dp')
- d_expert_bias: float32 [4, 1536], P('expert', 'dp')
- d_expert_out: float32 [4, 1536, 384], P('expert', 'dp')
Inputs may be any that keep to these rules, and one draw needn't show every extreme that they name: `expert_index`: each token names two different experts. `expert_slot`: in each micro-batch and each aligned block of 1 images, the kept routes to one expert take the slots 0, 1, 2 and so on in token order, a token's first expert before its second, without gaps or repeats; a dropped route has slot 0. In every micro-batch one expert has all 128 slots taken in every block. `route_kept`: in each micro-batch and each aligned block of 1 images, a route is kept exactly when fewer than 128 earlier routes of the block, in that order, go to the same expert; every block drops some routes.
All inputs are finite; a program needn't handle non-finite values.
Results may differ from a plain program's by a relative error of at most 0.024.
Values may be sent and summed in bfloat16 or wider, within the bound.
No kernel may reach another device: no remote copies, remote signals or barrier semaphores. Data moves between devices by JAX's collectives and lax.ppermute only.
A program may use at most 128 MiB of HBM per device.

v0:
```python
import jax
import jax.numpy as jnp
from jax import lax
from jax.sharding import PartitionSpec as P

HEADS = 6
HEAD_DIM = 64
D = 384
SEQ = 197
IMG_DEV = 1
MB = 3


EPSILON = 1e-06


def for_sending(value):
    return jax.tree.map(lambda a: a.astype(jnp.bfloat16) if a.dtype == jnp.float32 else a, value)


def layer_norm(values, gain):
    centre = jnp.mean(values, axis=-1, keepdims=True)
    centered = values - centre
    spread = jnp.mean(centered * centered, axis=-1, keepdims=True)
    return centered * lax.rsqrt(spread + EPSILON) * gain


def exact_gelu(values):
    return jax.nn.gelu(values, approximate=False)


def body(
    tokens,
    expert_index,
    expert_slot,
    route_kept,
    ln1_gain,
    w_qkv,
    w_out,
    ln2_gain,
    w_router,
    expert_in,
    expert_bias,
    expert_out,
    cotangent,
):
    local_experts = expert_in.shape[0]
    group_count = lax.axis_size("expert")
    expert_count = group_count * local_experts
    capacity = 8 * (5 * IMG_DEV * SEQ // (16 * expert_count) + 1)
    token_rows = IMG_DEV * SEQ
    scale = HEAD_DIM ** (-0.5)
    highest = lax.Precision.HIGHEST

    def fetch_dense():
        return (
            lax.all_gather(ln1_gain, "dp", axis=0, tiled=True),
            lax.all_gather(w_qkv, "dp", axis=0, tiled=True),
            lax.all_gather(w_out, "dp", axis=0, tiled=True),
            lax.all_gather(ln2_gain, "dp", axis=0, tiled=True),
            lax.all_gather(w_router, "dp", axis=0, tiled=True),
        )

    def fetch_experts():
        return (
            lax.all_gather(expert_in, "dp", axis=1, tiled=True),
            lax.all_gather(expert_bias, "dp", axis=1, tiled=True),
            lax.all_gather(expert_out, "dp", axis=1, tiled=True),
        )

    kept_state = []
    outputs = []
    for micro_batch in range(MB):
        dense_all = fetch_dense()
        expert_all = fetch_experts()
        gain_one, packed_w, out_w, gain_two, router_w = dense_all
        first_w, first_bias, second_w = expert_all
        inputs = tokens[micro_batch].reshape(token_rows, D).astype(jnp.float32)
        normed = layer_norm(inputs, gain_one.astype(jnp.float32))
        normed_low = normed.astype(jnp.bfloat16)
        packed = jnp.dot(normed_low, packed_w, preferred_element_type=jnp.float32).astype(
            jnp.bfloat16
        )
        head_split = packed.reshape(IMG_DEV, SEQ, 3, HEADS, HEAD_DIM)
        query = head_split[:, :, 0]
        keyed = head_split[:, :, 1]
        valued = head_split[:, :, 2]
        scores = (
            jnp.einsum("iqhd,ikhd->ihqk", query, keyed, preferred_element_type=jnp.float32) * scale
        )
        score_top = jnp.max(scores, axis=-1, keepdims=True)
        log_total = score_top + jnp.log(
            jnp.sum(jnp.exp(scores - score_top), axis=-1, keepdims=True)
        )
        attn_low = jnp.exp(scores - log_total).astype(jnp.bfloat16)
        attended = (
            jnp.einsum("ihqk,ikhd->iqhd", attn_low, valued, preferred_element_type=jnp.float32)
            .reshape(token_rows, D)
            .astype(jnp.bfloat16)
        )
        middle = inputs + jnp.dot(attended, out_w, preferred_element_type=jnp.float32)
        normed_two = layer_norm(middle, gain_two.astype(jnp.float32))
        router = jax.nn.softmax(
            jnp.dot(normed_two, router_w.astype(jnp.float32), precision=highest), axis=-1
        )
        route_expert = expert_index[micro_batch].reshape(token_rows, 2)
        route_live = route_kept[micro_batch].reshape(token_rows, 2)
        live_float = route_live.astype(jnp.float32)
        route_target = route_expert * capacity + expert_slot[micro_batch].reshape(token_rows, 2)
        placed = jnp.where(route_live > 0, route_target, expert_count * capacity).reshape(-1)
        fetched = jnp.where(route_live > 0, route_target, 0).reshape(-1)
        one_hot = (
            route_expert[:, :, None] == jnp.arange(expert_count, dtype=jnp.int32)[None, None, :]
        ).astype(jnp.float32)
        gates = jnp.sum(one_hot * router[:, None, :], axis=-1) * live_float
        sending = (
            jnp.zeros((expert_count * capacity, D), jnp.bfloat16)
            .at[placed]
            .set(jnp.repeat(normed_two.astype(jnp.bfloat16), 2, axis=0), mode="drop")
        )
        received = lax.all_to_all(
            sending.reshape(group_count, local_experts, capacity, D),
            "expert",
            split_axis=0,
            concat_axis=0,
            tiled=True,
        )
        hidden = (
            jnp.einsum("necd,edf->necf", received, first_w, preferred_element_type=jnp.float32)
            + first_bias.astype(jnp.float32)[None, :, None, :]
        )
        expert_active = exact_gelu(hidden).astype(jnp.bfloat16)
        result = jnp.einsum(
            "necf,efd->necd", expert_active, second_w, preferred_element_type=jnp.float32
        ).astype(jnp.bfloat16)
        results, hidden, received = (result, hidden, received)
        returned = lax.all_to_all(
            results, "expert", split_axis=0, concat_axis=0, tiled=True
        ).reshape(expert_count * capacity, D)
        picked = returned[fetched].reshape(token_rows, 2, D)
        mixed = middle + jnp.sum(gates[:, :, None] * picked.astype(jnp.float32), axis=1)
        outputs.append(mixed.astype(jnp.bfloat16).reshape(IMG_DEV, SEQ, D))
        kept_state.append(
            (
                inputs,
                normed_low,
                query,
                keyed,
                valued,
                log_total,
                attended,
                middle,
                normed_two,
                router,
                one_hot,
                gates,
                live_float,
                placed,
                fetched,
                picked,
                received,
                hidden,
            )
        )
    dense_grads = None
    expert_grads = None
    token_grads = [None] * MB
    for micro_batch in reversed(range(MB)):
        dense_all = fetch_dense()
        expert_all = fetch_experts()
        gain_one, packed_w, out_w, gain_two, router_w = dense_all
        first_w, first_bias, second_w = expert_all
        gain_first = gain_one.astype(jnp.float32)
        gain_second = gain_two.astype(jnp.float32)
        router_full = router_w.astype(jnp.float32)
        (
            inputs,
            normed_low,
            query,
            keyed,
            valued,
            log_total,
            attended,
            middle,
            normed_two,
            router,
            one_hot,
            gates,
            live_float,
            placed,
            fetched,
            picked,
            received,
            hidden,
        ) = kept_state[micro_batch]
        grad_out = cotangent[micro_batch].reshape(token_rows, D).astype(jnp.float32)
        grad_picked = (gates[:, :, None] * grad_out[:, None, :]).astype(jnp.bfloat16)
        grad_gates = (
            jnp.sum(grad_out[:, None, :] * picked.astype(jnp.float32), axis=-1) * live_float
        )
        grad_router = jnp.sum(one_hot * grad_gates[:, :, None], axis=1)
        grad_logits = router * (grad_router - jnp.sum(router * grad_router, axis=-1, keepdims=True))
        grad_sending = (
            jnp.zeros((expert_count * capacity, D), jnp.bfloat16)
            .at[placed]
            .set(grad_picked.reshape(2 * token_rows, D), mode="drop")
        )
        grad_received = lax.all_to_all(
            grad_sending.reshape(group_count, local_experts, capacity, D),
            "expert",
            split_axis=0,
            concat_axis=0,
            tiled=True,
        )
        grad_active = jnp.einsum(
            "necd,efd->necf", grad_received, second_w, preferred_element_type=jnp.float32
        )
        active = exact_gelu(hidden).astype(jnp.bfloat16)
        grad_second = jnp.einsum(
            "necf,necd->efd", active, grad_received, preferred_element_type=jnp.float32
        )
        gelu_value, gelu_back = jax.vjp(exact_gelu, hidden)
        grad_hidden = gelu_back(grad_active)[0].astype(jnp.bfloat16)
        grad_first = jnp.einsum(
            "necd,necf->edf", received, grad_hidden, preferred_element_type=jnp.float32
        )
        grad_bias = jnp.sum(grad_hidden.astype(jnp.float32), axis=(0, 2))
        grad_inbox = jnp.einsum(
            "necf,edf->necd", grad_hidden, first_w, preferred_element_type=jnp.float32
        ).astype(jnp.bfloat16)
        grad_returned = lax.all_to_all(
            grad_inbox, "expert", split_axis=0, concat_axis=0, tiled=True
        ).reshape(expert_count * capacity, D)
        grad_routed = jnp.sum(
            grad_returned[fetched].reshape(token_rows, 2, D).astype(jnp.float32)
            * live_float[:, :, None],
            axis=1,
        )
        grad_normed_two = (
            jnp.einsum("re,de->rd", grad_logits, router_full, precision=highest) + grad_routed
        )
        grad_router_w = jnp.einsum("rd,re->de", normed_two, grad_logits, precision=highest)
        norm_value, norm_back = jax.vjp(layer_norm, middle, gain_second)
        grad_middle, grad_gain_two = norm_back(grad_normed_two)
        grad_middle = grad_middle + grad_out
        grad_branch = grad_middle.astype(jnp.bfloat16)
        grad_out_w = jnp.einsum(
            "rc,rd->cd", attended, grad_branch, preferred_element_type=jnp.float32
        )
        grad_attended = (
            jnp.einsum("rd,cd->rc", grad_branch, out_w, preferred_element_type=jnp.float32)
            .astype(jnp.bfloat16)
            .reshape(IMG_DEV, SEQ, HEADS, HEAD_DIM)
        )
        scores = (
            jnp.einsum("iqhd,ikhd->ihqk", query, keyed, preferred_element_type=jnp.float32) * scale
        )
        attn_float = jnp.exp(scores - log_total)
        attn_low = attn_float.astype(jnp.bfloat16)
        grad_weights = jnp.einsum(
            "iqhd,ikhd->ihqk", grad_attended, valued, preferred_element_type=jnp.float32
        )
        grad_valued = jnp.einsum(
            "ihqk,iqhd->ikhd", attn_low, grad_attended, preferred_element_type=jnp.float32
        )
        grad_scores = (
            attn_float * (grad_weights - jnp.sum(attn_float * grad_weights, axis=-1, keepdims=True))
        ).astype(jnp.bfloat16)
        grad_query = (
            jnp.einsum("ihqk,ikhd->iqhd", grad_scores, keyed, preferred_element_type=jnp.float32)
            * scale
        )
        grad_keyed = (
            jnp.einsum("ihqk,iqhd->ikhd", grad_scores, query, preferred_element_type=jnp.float32)
            * scale
        )
        grad_packed = (
            jnp.stack([grad_query, grad_keyed, grad_valued], axis=2)
            .reshape(token_rows, 3 * D)
            .astype(jnp.bfloat16)
        )
        grad_normed = jnp.einsum(
            "rc,dc->rd", grad_packed, packed_w, preferred_element_type=jnp.float32
        )
        grad_packed_w = jnp.einsum(
            "rd,rc->dc", normed_low, grad_packed, preferred_element_type=jnp.float32
        )
        norm_first, norm_back_first = jax.vjp(layer_norm, inputs, gain_first)
        grad_inputs, grad_gain_one = norm_back_first(grad_normed)
        token_grads[micro_batch] = (grad_middle + grad_inputs).reshape(IMG_DEV, SEQ, D)
        dense_step = (grad_gain_one, grad_packed_w, grad_out_w, grad_gain_two, grad_router_w)
        expert_step = (grad_first, grad_bias, grad_second)
        if dense_grads is None:
            dense_grads = dense_step
            expert_grads = expert_step
        else:
            dense_grads = jax.tree.map(lambda total, extra: total + extra, dense_grads, dense_step)
            expert_grads = jax.tree.map(
                lambda total, extra: total + extra, expert_grads, expert_step
            )
    summed = jax.tree.map(
        lambda part: part.astype(jnp.float32), lax.psum(for_sending(dense_grads), "expert")
    )
    dense_shares = jax.tree.map(
        lambda part: part.astype(jnp.float32),
        lax.psum_scatter(for_sending(summed), "dp", scatter_dimension=0, tiled=True),
    )
    expert_shares = jax.tree.map(
        lambda part: part.astype(jnp.float32),
        lax.psum_scatter(for_sending(expert_grads), "dp", scatter_dimension=1, tiled=True),
    )
    output = jnp.stack(outputs, axis=0)
    d_tokens = jnp.stack(token_grads, axis=0)
    return (
        output,
        d_tokens,
        dense_shares[0],
        dense_shares[1],
        dense_shares[2],
        dense_shares[3],
        dense_shares[4],
        expert_shares[0],
        expert_shares[1],
        expert_shares[2],
    )


def solution(mesh):
    placed = (
        P(None, ("dp", "expert"), None, None),
        P(None, ("dp", "expert"), None, None),
        P(None, ("dp", "expert"), None, None),
        P(None, ("dp", "expert"), None, None),
        P("dp"),
        P("dp", None),
        P("dp", None),
        P("dp"),
        P("dp", None),
        P("expert", "dp", None),
        P("expert", "dp"),
        P("expert", "dp", None),
        P(None, ("dp", "expert"), None, None),
    )
    return jax.shard_map(
        body,
        mesh=mesh,
        in_specs=placed,
        out_specs=(
            P(None, ("dp", "expert"), None, None),
            P(None, ("dp", "expert"), None, None),
            P("dp"),
            P("dp", None),
            P("dp", None),
            P("dp"),
            P("dp", None),
            P("expert", "dp", None),
            P("expert", "dp"),
            P("expert", "dp", None),
        ),
        check_vma=False,
    )
```

profile of v0, /device:TPU:0, one launch (start us, length us, event | category | flops | bytes accessed | tf_op | source)
XLA Modules:
  0.0 862.5 jit_solution(536602558780141070)
XLA Ops:
  7.9 34.9 %all_gather.17 = bf16[384,1152]{1,0:T(8,128)(2,1)S(1)} all-gather(bf16[48,1152]{1,0:T(8,128)(2,1)} %param.18), channel_id=1, replica_groups=mesh['dp'=8,'expert'=4] {'dp'}, dimensions={0}, use_global_device_ids=true | all-gather | bytes 995328 | tf_op jit(solution)/shard_map/all_gather | solution.py:58
  48.1 21.8 %all-reduce.6 = (bf16[1536]{0:T(1024)(128)(2,1)}, bf16[384]{0:T(512)(128)(2,1)S(1)}, bf16[384]{0:T(512)(128)(2,1)S(1)}) all-reduce(bf16[1536]{0:T(1024)(128)(2,1)S(1)} %dynamic-update-slice.2, bf16[384]{0:T(512)(128)(2,1)S(1)} %dynamic-update-slice, bf16[384]{0:T(512)(128)(2,1)S(1)} %dynamic-update-slice.1), channel_id=1, replica_groups=mesh['dp'=8,'expert'=4] {'dp'}, use_global_device_ids=true, to_apply=%add.2 | all-reduce | flops 2304 | bytes 9216
  71.2 31.0 %all_gather.18 = bf16[384,384]{1,0:T(8,128)(2,1)S(1)} all-gather(bf16[48,384]{1,0:T(8,128)(2,1)} %param.19), channel_id=1, replica_groups=mesh['dp'=8,'expert'=4] {'dp'}, dimensions={0}, use_global_device_ids=true | all-gather | bytes 331776 | tf_op jit(solution)/shard_map/all_gather | solution.py:59
  131.8 17.0 %all-gather = bf16[8,48,4]{1,2,0:T(4,128)(2,1)S(1)} all-gather(bf16[1,48,4]{1,2,0:T(4,128)(2,1)} %bitcast.884), channel_id=1, replica_groups=mesh['dp'=8,'expert'=4] {'dp'}, dimensions={0}, use_global_device_ids=true | all-gather | bytes 3456 | tf_op jit(solution)/shard_map/all_gather | solution.py:61
  216.9 4.6 all-to-all-start.2
  225.6 7.8 fusion.75
  241.5 7.7 fusion.76
  253.5 7.0 convert_reduce_fusion
  262.2 4.1 all-to-all-start.3
  266.3 7.0 convert_reduce_fusion.1
  275.1 4.3 all-to-all-start.1
  290.6 4.1 all-to-all-start.7
  382.3 7.8 fusion.77
  390.1 5.8 convert_reduce_fusion.2
  458.4 42.4 %reduce-scatter.15.cloned.1.call-done = bf16[48,1152]{1,0:T(8,128)(2,1)} async-done(((bf16[384,1152]{1,0:T(8,128)(2,1)}), bf16[48,1152]{1,0:T(8,128)(2,1)}) %reduce-scatter.15.cloned.1.call-update) | async-done | bytes 110608 | tf_op jit(solution)/shard_map/reduce_scatter | solution.py:306
  500.9 4.7 fusion.73
  513.6 51.2 %reduce-scatter.19.cloned.1.call-done = bf16[192,1]{1,0:T(8,128)(2,1)} async-done(((bf16[1536,1]{1,0:T(8,128)(2,1)}), bf16[192,1]{1,0:T(8,128)(2,1)}) %reduce-scatter.19.cloned.1.call-update) | async-done | bytes 400
  571.2 19.5 %all-reduce.5 = (bf16[384]{0:T(512)(128)(2,1)S(1)}, bf16[384]{0:T(512)(128)(2,1)S(1)}) all-reduce(bf16[384]{0:T(512)(128)(2,1)S(1)} %add_convert_fusion.5, bf16[384]{0:T(512)(128)(2,1)S(1)} %add_convert_fusion.4), channel_id=2, replica_groups=mesh['dp'=8,'expert'=4] {'dp'}, use_global_device_ids=true, to_apply=%region_67.68.clone | all-reduce | flops 768 | bytes 3072
  591.7 33.5 %reduce-scatter.21.cloned.1.call-done = bf16[48,4]{1,0:T(8,128)(2,1)} async-done(((bf16[384,4]{1,0:T(8,128)(2,1)}), bf16[48,4]{1,0:T(8,128)(2,1)}) %reduce-scatter.21.cloned.1.call-update) | async-done | bytes 400
  625.9 60.7 %reduce-scatter.17.cloned.1.call-done = bf16[48,384]{1,0:T(8,128)(2,1)} async-done(((bf16[384,384]{1,0:T(8,128)(2,1)}), bf16[48,384]{1,0:T(8,128)(2,1)}) %reduce-scatter.17.cloned.1.call-update) | async-done | bytes 36880 | tf_op jit(solution)/shard_map/reduce_scatter | solution.py:306
  686.7 11.0 %all-reduce.7 = (bf16[48]{0:T(256)(128)(2,1)S(1)}, bf16[48,384]{1,0:T(8,128)(2,1)S(1)}, bf16[48]{0:T(256)(128)(2,1)S(1)}, bf16[48,4]{0,1:T(4,128)(2,1)S(1)}) all-reduce(bf16[48]{0:T(256)(128)(2,1)S(1)} %dynamic-slice.4, bf16[48,384]{1,0:T(8,128)(2,1)} %reduce-scatter.17.cloned.1.call-done, ...), channel_id=1, replica_groups=mesh['dp'=8,'expert'=4] {'expert'}, use_global_device_ids=true, to_apply=%region_66.67 | all-reduce | flops 18720 | bytes 74880 | tf_op jit(solution)/shard_map/psum | solution.py:302
  699.9 18.0 %all-reduce.10.cloned.1.call-done = bf16[48,1152]{1,0:T(8,128)(2,1)} async-done(((bf16[48,1152]{1,0:T(8,128)(2,1)}), bf16[48,1152]{1,0:T(8,128)(2,1)}) %all-reduce.10.cloned.1.call-update) | async-done | bytes 110608 | tf_op jit(solution)/shard_map/psum | solution.py:302
  719.5 67.7 %reduce-scatter.11.cloned.1.call-done = bf16[1,48,1536]{2,1,0:T(8,128)(2,1)} async-done(((bf16[1,384,1536]{2,1,0:T(8,128)(2,1)}), bf16[1,48,1536]{2,1,0:T(8,128)(2,1)}) %reduce-scatter.11.cloned.1.call-update) | async-done | bytes 147472 | tf_op jit(solution)/shard_map/reduce_scatter | solution.py:310
  788.9 65.1 %reduce-scatter.13.cloned.1.call-done = bf16[1,192,384]{2,1,0:T(8,128)(2,1)} async-done(((bf16[1,1536,384]{2,1,0:T(8,128)(2,1)}), bf16[1,192,384]{2,1,0:T(8,128)(2,1)}) %reduce-scatter.13.cloned.1.call-update) | async-done | bytes 147472 | tf_op jit(solution)/shard_map/reduce_scatter | solution.py:310
  (614 shorter events, 305.0 us)
Async XLA Ops:
  7.2 214.4 %all-gather.4.cloned.1.call-start = ((), (), s32[]{:S(2)}) async-start(), calls=%async_computation.18 | async-start | bytes 1327104 | tf_op jit(solution)/shard_map/all_gather | solution.py:66
  125.8 91.2 %all-to-all-start = ((bf16[4,1,128,384]{3,2,1,0:T(8,128)(2,1)}), bf16[4,1,128,384]{3,2,1,0:T(8,128)(2,1)}, u32[]{:S(2)}, u32[]{:S(2)}) async-start(bf16[4,1,128,384]{3,2,1,0:T(8,128)(2,1)} %bitcast.870), calls=%async_computation | async-start | bytes 786432 | tf_op jit(solution)/shard_map/all_to_all | solution.py:121
  129.9 123.6 %all-gather.6.cloned.1.call-start = ((), (), s32[]{:S(2)}) async-start(), calls=%async_computation.19 | async-start | bytes 1327104 | tf_op jit(solution)/shard_map/all_gather | solution.py:68
  216.9 16.5 %all-to-all-start.2 = ((bf16[4,1,128,384]{3,2,1,0:T(8,128)(2,1)}), bf16[4,1,128,384]{3,2,1,0:T(8,128)(2,1)}, u32[]{:S(2)}, u32[]{:S(2)}) async-start(bf16[4,1,128,384]{3,2,1,0:T(8,128)(2,1)} %bitcast.873), calls=%async_computation.2 | async-start | bytes 786432 | tf_op jit(solution)/shard_map/all_to_all | solution.py:121
  233.4 15.9 %all-to-all-start.6 = ((bf16[4,1,128,384]{3,2,1,0:T(8,128)(2,1)}), bf16[4,1,128,384]{3,2,1,0:T(8,128)(2,1)}, u32[]{:S(2)}, u32[]{:S(2)}) async-start(bf16[4,1,128,384]{3,2,1,0:T(8,128)(2,1)} %bitcast.872), calls=%async_computation.6 | async-start | bytes 786432 | tf_op jit(solution)/shard_map/all_to_all | solution.py:208
  249.3 12.9 %all-to-all-start.8 = ((bf16[4,1,128,384]{3,2,1,0:T(8,128)(2,1)}), bf16[4,1,128,384]{3,2,1,0:T(8,128)(2,1)}, u32[]{:S(2)}, u32[]{:S(2)}) async-start(bf16[4,1,128,384]{3,2,1,0:T(8,128)(2,1)} %bitcast.871), calls=%async_computation.8 | async-start | bytes 786432 | tf_op jit(solution)/shard_map/all_to_all | solution.py:208
  262.2 12.9 %all-to-all-start.3 = ((bf16[4,1,128,384]{3,2,1,0:T(8,128)(2,1)}), bf16[4,1,128,384]{3,2,1,0:T(8,128)(2,1)}, u32[]{:S(2)}, u32[]{:S(2)}) async-start(bf16[4,1,128,384]{3,2,1,0:T(8,128)(2,1)} %fusion.98), calls=%async_computation.3 | async-start | bytes 786432 | tf_op jit(solution)/shard_map/all_to_all | solution.py:137
  275.1 15.5 %all-to-all-start.1 = ((bf16[4,1,128,384]{3,2,1,0:T(8,128)(2,1)}), bf16[4,1,128,384]{3,2,1,0:T(8,128)(2,1)}, u32[]{:S(2)}, u32[]{:S(2)}) async-start(bf16[4,1,128,384]{3,2,1,0:T(8,128)(2,1)} %fusion.97), calls=%async_computation.1 | async-start | bytes 786432 | tf_op jit(solution)/shard_map/all_to_all | solution.py:137
  290.6 18.6 %all-to-all-start.7 = ((bf16[4,1,128,384]{3,2,1,0:T(8,128)(2,1)}), bf16[4,1,128,384]{3,2,1,0:T(8,128)(2,1)}, u32[]{:S(2)}, u32[]{:S(2)}) async-start(bf16[4,1,128,384]{3,2,1,0:T(8,128)(2,1)} %fusion.106), calls=%async_computation.7 | async-start | bytes 786432 | tf_op jit(solution)/shard_map/all_to_all | solution.py:231
  309.1 13.8 %all-to-all-start.9 = ((bf16[4,1,128,384]{3,2,1,0:T(8,128)(2,1)}), bf16[4,1,128,384]{3,2,1,0:T(8,128)(2,1)}, u32[]{:S(2)}, u32[]{:S(2)}) async-start(bf16[4,1,128,384]{3,2,1,0:T(8,128)(2,1)} %fusion.103), calls=%async_computation.9 | async-start | bytes 786432 | tf_op jit(solution)/shard_map/all_to_all | solution.py:231
  355.0 83.8 %copy-start.97 = (f32[197]{0:T(256)}, f32[197]{0:T(256)S(1)}, u32[]{:S(2)}) copy-start(f32[197]{0:T(256)S(1)} %fusion.294) | copy-start | bytes 2368
  364.0 10.9 %all-to-all-start.4 = ((bf16[4,1,128,384]{3,2,1,0:T(8,128)(2,1)}), bf16[4,1,128,384]{3,2,1,0:T(8,128)(2,1)S(1)}, u32[]{:S(2)}, u32[]{:S(2)}) async-start(bf16[4,1,128,384]{3,2,1,0:T(8,128)(2,1)} %bitcast.68), calls=%async_computation.4 | async-start | bytes 786432 | tf_op jit(solution)/shard_map/all_to_all | solution.py:121
  374.9 15.2 %all-to-all-start.10 = ((bf16[4,1,128,384]{3,2,1,0:T(8,128)(2,1)}), bf16[4,1,128,384]{3,2,1,0:T(8,128)(2,1)S(1)}, u32[]{:S(2)}, u32[]{:S(2)}) async-start(bf16[4,1,128,384]{3,2,1,0:T(8,128)(2,1)} %bitcast.135), calls=%async_computation.10 | async-start | bytes 786432 | tf_op jit(solution)/shard_map/all_to_all | solution.py:208
  398.9 11.0 %all-to-all-start.11 = ((bf16[4,1,128,384]{3,2,1,0:T(8,128)(2,1)}), bf16[4,1,128,384]{3,2,1,0:T(8,128)(2,1)S(1)}, u32[]{:S(2)}, u32[]{:S(2)}) async-start(bf16[4,1,128,384]{3,2,1,0:T(8,128)(2,1)} %fusion.100), calls=%async_computation.11 | async-start | bytes 786432 | tf_op jit(solution)/shard_map/all_to_all | solution.py:231
  409.9 10.9 %all-to-all-start.5 = ((bf16[4,1,128,384]{3,2,1,0:T(8,128)(2,1)}), bf16[4,1,128,384]{3,2,1,0:T(8,128)(2,1)S(1)}, u32[]{:S(2)}, u32[]{:S(2)}) async-start(bf16[4,1,128,384]{3,2,1,0:T(8,128)(2,1)} %fusion.99), calls=%async_computation.5 | async-start | bytes 786432 | tf_op jit(solution)/shard_map/all_to_all | solution.py:137
  413.3 87.4 %reduce-scatter.15.cloned.1.call-start = ((), (), s32[]{:S(2)}) async-start(), calls=%async_computation.22 | async-start | bytes 995328 | tf_op jit(solution)/shard_map/reduce_scatter | solution.py:306
  442.0 122.9 %reduce-scatter.19.cloned.1.call-start = ((), (), s32[]{:S(2)}) async-start(), calls=%async_computation.25 | async-start | bytes 442368
  443.1 182.1 %reduce-scatter.21.cloned.1.call-start = ((), (), s32[]{:S(2)}) async-start(), calls=%async_computation.26 | async-start | bytes 110592
  448.9 237.8 %reduce-scatter.17.cloned.1.call-start = ((), (), s32[]{:S(2)}) async-start(), calls=%async_computation.24 | async-start | bytes 331776 | tf_op jit(solution)/shard_map/reduce_scatter | solution.py:306
  451.2 266.7 %all-reduce.10.cloned.1.call-start = ((), (), s32[]{:S(2)}) async-start(), calls=%async_computation.23 | async-start | bytes 221184 | tf_op jit(solution)/shard_map/psum | solution.py:302
  500.8 286.4 %reduce-scatter.11.cloned.1.call-start = ((), (), s32[]{:S(2)}) async-start(), calls=%async_computation.20 | async-start | bytes 1327104 | tf_op jit(solution)/shard_map/reduce_scatter | solution.py:310
  505.6 348.5 %reduce-scatter.13.cloned.1.call-start = ((), (), s32[]{:S(2)}) async-start(), calls=%async_computation.21 | async-start | bytes 1327104 | tf_op jit(solution)/shard_map/reduce_scatter | solution.py:310
  513.6 55.2 %copy-start.113 = (f32[197]{0:T(256)S(1)}, f32[197]{0:T(256)}, u32[]{:S(2)}) copy-start(f32[197]{0:T(256)} %copy-done.111) | copy-start | bytes 2368
  513.6 55.2 %copy-start.116 = (f32[197]{0:T(256)S(1)}, f32[197]{0:T(256)}, u32[]{:S(2)}) copy-start(f32[197]{0:T(256)} %copy-done.114) | copy-start | bytes 2368
  (160 other events, 1623.9 us)
Sparse Core Ops, SparseCore 0:
  10.2 46.0 all-gather.3
  132.9 39.0 all-gather.5
  442.1 58.6 reduce-scatter.14
  504.5 60.2 reduce-scatter.18
  568.5 56.6 reduce-scatter.20
  628.9 57.7 reduce-scatter.16
  689.0 28.8 all-reduce.9
  721.7 65.5 reduce-scatter.10
  791.0 62.9 reduce-scatter.12
where the time goes:
time: 872 us; the launch traced here: 862 us
  waiting for transfers between devices  348 us (40%)
  blocking collectives  135 us (15%)
  local copies, waits for them, and re-layouts  120 us (14%)
  matrix products  104 us (12%)
  other arithmetic  87.8 us (10%)
  starting transfers between devices  48.4 us (6%)
  between operations  18.6 us (2%)
    reduce_scatter x2, waiting for transfers between devices, body(): lax.psum_scatter(for_sending(expert_grads), 'dp', scatter_dimension=1, ti...  133 us
    reduce_scatter x2, waiting for transfers between devices, body(): lax.psum_scatter(for_sending(summed), 'dp', scatter_dimension=0, tiled=True)  103 us
    unnamed x11, waiting for transfers between devices  86.2 us
    unnamed x2, blocking collectives  41.3 us
    all_gather x1, blocking collectives, fetch_dense(): lax.all_gather(w_qkv, 'dp', axis=0, tiled=True)  34.9 us
    all_gather x1, blocking collectives, fetch_dense(): lax.all_gather(w_out, 'dp', axis=0, tiled=True)  31 us
    another operation x3, other arithmetic  23.3 us
    unnamed x341, local copies, waits for them, and re-layouts  21.1 us
  transfers between devices with their start and end apart: 21, of which 10 were waited for; matrix products, arithmetic and copies ran while one was open for 27% of the time, Pallas kernels for 0%

commit v1 on v0

v1 whole, which is shorter than its diff:
```python
import functools

import jax
import jax.numpy as jnp
from jax import lax
from jax.experimental import pallas as pl
from jax.experimental.pallas import tpu as pltpu
from jax.sharding import PartitionSpec as P

HEADS = 6
HEAD_DIM = 64
D = 384
SEQ = 197
MB = 3
LANES = 128
EPSILON = 1e-06
HIGHEST = lax.Precision.HIGHEST
VMEM_BYTES = 48 * 1024 * 1024
bf16 = jnp.bfloat16
f32 = jnp.float32


def dot(a, b, ca=1, cb=0, precision=None):
    return lax.dot_general(
        a, b, (((ca,), (cb,)), ((), ())), precision=precision, preferred_element_type=f32
    )


def xor_pairs(n, k):
    return [(i, i ^ k) for i in range(n)]


def spread_of(values):
    centre = jnp.mean(values, axis=-1, keepdims=True)
    centered = values - centre
    spread = jnp.mean(centered * centered, axis=-1, keepdims=True)
    rate = lax.rsqrt(spread + EPSILON)
    return centered * rate, rate


def norm_back(grad_hat, hat, rate):
    mean_one = jnp.mean(grad_hat, axis=-1, keepdims=True)
    mean_two = jnp.mean(grad_hat * hat, axis=-1, keepdims=True)
    return rate * (grad_hat - mean_one - hat * mean_two)


def side_rows(dense_ref):
    return jnp.transpose(dense_ref[:, 4 * D :].astype(f32))


def route_masks(index_ref, slot_ref, kept_ref, me, groups, capacity):
    index = index_ref[0, 0]
    target = jnp.where(kept_ref[0, 0] > 0, (index ^ me) * capacity + slot_ref[0, 0], -1)
    lanes = lax.broadcasted_iota(jnp.int32, (SEQ, groups * capacity), 1)
    places = [(lanes == target[:, k : k + 1]).astype(f32).astype(bf16) for k in range(2)]
    experts = lax.broadcasted_iota(jnp.int32, (SEQ, groups), 1)
    chosen = [(experts == index[:, k : k + 1]).astype(f32) for k in range(2)]
    return places, chosen


def half_mask(which):
    lanes = lax.broadcasted_iota(jnp.int32, (SEQ, LANES), 1)
    return (lanes < HEAD_DIM) if which == 0 else (lanes >= HEAD_DIM)


def forward_kernel(groups, capacity, me_ref, tokens_ref, index_ref, slot_ref, kept_ref, cot_ref, dense_ref, packed_ref, attn_ref, attended_ref, middle_ref, router_ref, *sends):
    me = me_ref[0]
    side = side_rows(dense_ref)
    gain_one = side[groups : groups + 1]
    gain_two = side[groups + 1 : groups + 2]
    inputs = tokens_ref[0, 0].astype(f32)
    hat, _ = spread_of(inputs)
    normed_low = (hat * gain_one).astype(bf16)
    packed = dot(normed_low, dense_ref[:, : 3 * D]).astype(bf16)
    packed_ref[...] = packed
    scale = HEAD_DIM ** (-0.5)
    parts = []
    for pair in range(HEADS // 2):
        lo = pair * LANES
        query = packed[:, lo : lo + LANES]
        keyed = packed[:, D + lo : D + lo + LANES]
        valued = packed[:, 2 * D + lo : 2 * D + lo + LANES]
        outs = []
        for which in range(2):
            masked = jnp.where(half_mask(which), query, jnp.zeros_like(query))
            scores = dot(masked, keyed, 1, 1) * scale
            top = jnp.max(scores, axis=-1, keepdims=True)
            raised = jnp.exp(scores - top)
            total = jnp.sum(raised, axis=-1, keepdims=True)
            attn_low = (raised * (1.0 / total)).astype(bf16)
            attn_ref[2 * pair + which] = attn_low
            outs.append(dot(attn_low, valued))
        parts.append(jnp.where(half_mask(0), outs[0], outs[1]))
    attended = jnp.concatenate(parts, axis=1).astype(bf16)
    attended_ref[...] = attended
    middle = inputs + dot(attended, dense_ref[:, 3 * D : 4 * D])
    middle_ref[...] = middle
    hat_two, _ = spread_of(middle)
    normed_two = hat_two * gain_two
    router_w = dense_ref[:, 4 * D :].astype(f32)[:, :groups]
    logits = dot(normed_two, router_w, precision=HIGHEST)
    raised = jnp.exp(logits - jnp.max(logits, axis=-1, keepdims=True))
    router = raised / jnp.sum(raised, axis=-1, keepdims=True)
    router_ref[...] = router
    places, chosen = route_masks(index_ref, slot_ref, kept_ref, me, groups, capacity)
    cot = cot_ref[0, 0].astype(f32)
    inbox = dot(places[0] + places[1], normed_two.astype(bf16), 0, 0).astype(bf16)
    grad_outbox = jnp.zeros((groups * capacity, D), f32)
    for k in range(2):
        gate = jnp.sum(chosen[k] * router, axis=-1, keepdims=True)
        grad_outbox += dot(places[k], (gate * cot).astype(bf16), 0, 0)
    grad_outbox = grad_outbox.astype(bf16)
    for g in range(groups):
        sends[g][:capacity] = inbox[g * capacity : (g + 1) * capacity]
        sends[g][capacity:] = grad_outbox[g * capacity : (g + 1) * capacity]


def expert_kernel(groups, capacity, *refs):
    boxes = refs[:groups]
    first_ref, bias_ref, second_ref = refs[groups : groups + 3]
    backs = refs[groups + 3 : 2 * groups + 3]
    active_ref, grad_hidden_ref = refs[2 * groups + 3 :]
    inbox = jnp.concatenate([box[:capacity] for box in boxes], axis=0)
    grad_outbox = jnp.concatenate([box[capacity:] for box in boxes], axis=0)
    wide = first_ref.shape[1]
    step = wide // 3
    outbox = jnp.zeros((groups * capacity, D), f32)
    grad_inbox = jnp.zeros((groups * capacity, D), f32)
    for at in range(0, wide, step):
        first = first_ref[:, at : at + step]
        second = second_ref[at : at + step, :]
        hidden = dot(inbox, first) + bias_ref[:, at : at + step].astype(f32)
        cdf = 0.5 + 0.5 * lax.erf(hidden * (0.5**0.5))
        density = jnp.exp(hidden * hidden * (-0.5)) * 0.3989422804014327
        active = (hidden * cdf).astype(bf16)
        grad_active = dot(grad_outbox, second, 1, 1)
        grad_hidden = ((cdf + hidden * density) * grad_active).astype(bf16)
        active_ref[:, at : at + step] = active
        grad_hidden_ref[:, at : at + step] = grad_hidden
        outbox += dot(active, second)
        grad_inbox += dot(grad_hidden, first, 1, 1)
    outbox = outbox.astype(bf16)
    grad_inbox = grad_inbox.astype(bf16)
    for g in range(groups):
        backs[g][:capacity] = outbox[g * capacity : (g + 1) * capacity]
        backs[g][capacity:] = grad_inbox[g * capacity : (g + 1) * capacity]


def second_grad_kernel(groups, capacity, owners, *refs):
    boxes = [refs[m * groups : (m + 1) * groups] for m in range(MB)]
    actives = refs[MB * groups : MB * groups + MB]
    out_ref = refs[-1]
    rows = out_ref.shape[1]
    grads = [
        jnp.concatenate([box[capacity:] for box in boxes[m]], axis=0) for m in range(MB)
    ]
    wide = owners * rows
    step = wide // 3 if (wide // 3) % rows == 0 else wide // 2
    for at in range(0, wide, step):
        total = dot(actives[0][:, at : at + step], grads[0], 0, 0)
        for m in range(1, MB):
            total += dot(actives[m][:, at : at + step], grads[m], 0, 0)
        total = total.astype(bf16)
        for j in range(step // rows):
            out_ref[at // rows + j] = total[j * rows : (j + 1) * rows]


def first_grad_kernel(groups, capacity, owners, *refs):
    boxes = [refs[m * groups : (m + 1) * groups] for m in range(MB)]
    hiddens = refs[MB * groups : MB * groups + MB]
    out_ref = refs[-1]
    rows = D // owners
    extra = out_ref.shape[1] - rows
    inboxes = [
        jnp.concatenate([box[:capacity] for box in boxes[m]], axis=0) for m in range(MB)
    ]
    wide = out_ref.shape[2]
    step = wide // 3
    for at in range(0, wide, step):
        total = dot(inboxes[0], hiddens[0][:, at : at + step], 0, 0)
        bias = jnp.sum(hiddens[0][:, at : at + step].astype(f32), axis=0, keepdims=True)
        for m in range(1, MB):
            total += dot(inboxes[m], hiddens[m][:, at : at + step], 0, 0)
            bias += jnp.sum(hiddens[m][:, at : at + step].astype(f32), axis=0, keepdims=True)
        total = total.astype(bf16)
        bias = jnp.broadcast_to(bias, (extra, step)).astype(bf16)
        for j in range(owners):
            out_ref[j, :rows, at : at + step] = total[j * rows : (j + 1) * rows]
            out_ref[j, rows:, at : at + step] = bias


def backward_kernel(groups, capacity, has_total, me_ref, tokens_ref, index_ref, slot_ref, kept_ref, cot_ref, dense_ref, packed_ref, attn_ref, attended_ref, middle_ref, router_ref, *refs):
    backs = refs[:groups]
    total_ref = refs[groups] if has_total else None
    output_ref, d_tokens_ref, grads_ref = refs[-3:]
    me = me_ref[0]
    side = side_rows(dense_ref)
    gain_one = side[groups : groups + 1]
    gain_two = side[groups + 1 : groups + 2]
    middle = middle_ref[...]
    router = router_ref[...]
    cot = cot_ref[0, 0].astype(f32)
    places, chosen = route_masks(index_ref, slot_ref, kept_ref, me, groups, capacity)
    outbox = jnp.concatenate([box[:capacity] for box in backs], axis=0)
    grad_inbox = jnp.concatenate([box[capacity:] for box in backs], axis=0)
    mixed = middle
    grad_router = jnp.zeros((SEQ, groups), f32)
    for k in range(2):
        picked = dot(places[k], outbox)
        gate = jnp.sum(chosen[k] * router, axis=-1, keepdims=True)
        mixed = mixed + gate * picked
        grad_router += chosen[k] * jnp.sum(cot * picked, axis=-1, keepdims=True)
    output_ref[0] = mixed.astype(bf16)
    grad_logits = router * (grad_router - jnp.sum(router * grad_router, axis=-1, keepdims=True))
    router_w = dense_ref[:, 4 * D :].astype(f32)[:, :groups]
    grad_normed_two = dot(grad_logits, router_w, 1, 1, precision=HIGHEST) + dot(
        places[0] + places[1], grad_inbox
    )
    hat_two, rate_two = spread_of(middle)
    grad_middle = norm_back(grad_normed_two * gain_two, hat_two, rate_two) + cot
    lanes = lax.broadcasted_iota(jnp.int32, (SEQ, LANES), 1)
    column_one = (lanes == groups).astype(f32)
    column_two = (lanes == groups + 1).astype(f32)
    logits_wide = sum(
        jnp.where(lanes == e, grad_logits[:, e : e + 1], 0.0) for e in range(groups)
    )
    side_grad = dot(hat_two * gain_two, logits_wide, 0, 0, precision=HIGHEST)
    side_grad += dot(grad_normed_two * hat_two, column_two, 0, 0, precision=HIGHEST)
    grad_branch = grad_middle.astype(bf16)
    out_grad = dot(attended_ref[...], grad_branch, 0, 0)
    grad_attended = dot(grad_branch, dense_ref[:, 3 * D : 4 * D], 1, 1).astype(bf16)
    scale = HEAD_DIM ** (-0.5)
    first_half = half_mask(0)
    queries, keys, values = [], [], []
    for pair in range(HEADS // 2):
        lo = pair * LANES
        query = packed_ref[:, lo : lo + LANES]
        keyed = packed_ref[:, D + lo : D + lo + LANES]
        valued = packed_ref[:, 2 * D + lo : 2 * D + lo + LANES]
        pulled = grad_attended[:, lo : lo + LANES]
        q_outs, k_outs, v_outs = [], [], []
        for which in range(2):
            attn_low = attn_ref[2 * pair + which]
            attn = attn_low.astype(f32)
            masked = jnp.where(half_mask(which), pulled, jnp.zeros_like(pulled))
            weighted = dot(masked, valued, 1, 1)
            inner = jnp.sum(attn * weighted, axis=-1, keepdims=True)
            grad_scores = (attn * (weighted - inner)).astype(bf16)
            v_outs.append(dot(attn_low, pulled, 0, 0))
            q_outs.append(dot(grad_scores, keyed))
            k_outs.append(dot(grad_scores, query, 0, 0))
        queries.append(jnp.where(first_half, q_outs[0], q_outs[1]) * scale)
        keys.append(jnp.where(first_half, k_outs[0], k_outs[1]) * scale)
        values.append(jnp.where(first_half, v_outs[0], v_outs[1]))
    grad_packed = jnp.concatenate(queries + keys + values, axis=1).astype(bf16)
    grad_normed = dot(grad_packed, dense_ref[:, : 3 * D], 1, 1)
    hat, rate = spread_of(tokens_ref[0, 0].astype(f32))
    packed_grad = dot((hat * gain_one).astype(bf16), grad_packed, 0, 0)
    side_grad += dot(grad_normed * hat, column_one, 0, 0, precision=HIGHEST)
    d_tokens_ref[0] = grad_middle + norm_back(grad_normed * gain_one, hat, rate)
    for lo, part in ((0, packed_grad), (3 * D, out_grad), (4 * D, side_grad)):
        hi = lo + part.shape[1]
        if has_total:
            part = part + total_ref[:, lo:hi]
        grads_ref[:, lo:hi] = part


def arrange_kernel(count, me_ref, *refs):
    out_ref = refs[-1]
    for k in range(count):
        out_ref[me_ref[0] ^ k] = refs[k][...]


def params():
    return pltpu.CompilerParams(vmem_limit_bytes=VMEM_BYTES)


def whole(shape):
    zeros = (0,) * len(shape)
    return pl.BlockSpec(tuple(shape), lambda i: zeros)


def of_batch(shape, batch):
    tail = (0,) * (len(shape) - 1)
    return pl.BlockSpec((1,) + tuple(shape[1:]), lambda i: (batch,) + tail)


SCALAR = pl.BlockSpec(memory_space=pltpu.SMEM)


def call(kernel, name, in_specs, outs, args, flops, grid=(1,)):
    moved = sum(a.size * a.dtype.itemsize for a in args)
    moved += sum(a.size * a.dtype.itemsize for a in outs)
    return pl.pallas_call(
        kernel,
        grid=grid,
        in_specs=in_specs,
        out_specs=[whole(o.shape) for o in outs],
        out_shape=outs,
        compiler_params=params(),
        cost_estimate=pl.CostEstimate(flops=flops, bytes_accessed=moved, transcendentals=0),
        name=name,
    )(*args)


def like(shape, dtype):
    return jax.ShapeDtypeStruct(tuple(shape), dtype)


def gather_rows(piece, axis, me):
    count = lax.axis_size(axis)
    pieces = [piece] + [
        lax.ppermute(piece, axis, xor_pairs(count, k)) for k in range(1, count)
    ]
    out = call(
        functools.partial(arrange_kernel, count),
        "arrange",
        [SCALAR] + [whole(piece.shape)] * count,
        [like((count,) + piece.shape, piece.dtype)],
        [me] + pieces,
        0,
    )[0]
    return out.reshape((count * piece.shape[0],) + piece.shape[1:])


def scatter_sum(parts, axis, me):
    count = lax.axis_size(axis)
    total = lax.dynamic_index_in_dim(parts, me, 0, keepdims=False).astype(f32)
    for k in range(1, count):
        sent = lax.dynamic_index_in_dim(parts, me ^ k, 0, keepdims=False)
        total += lax.ppermute(sent, axis, xor_pairs(count, k)).astype(f32)
    return total


def body(
    tokens,
    expert_index,
    expert_slot,
    route_kept,
    ln1_gain,
    w_qkv,
    w_out,
    ln2_gain,
    w_router,
    expert_in,
    expert_bias,
    expert_out,
    cotangent,
):
    groups = lax.axis_size("expert")
    owners = lax.axis_size("dp")
    capacity = 8 * (5 * SEQ // (16 * groups) + 1)
    slots = groups * capacity
    wide = expert_in.shape[2]
    me_expert = lax.axis_index("expert")
    me_owner = lax.axis_index("dp")
    me_e = me_expert.reshape(1).astype(jnp.int32)
    me_o = me_owner.reshape(1).astype(jnp.int32)
    side_width = LANES
    rows = w_qkv.shape[0]
    side = jnp.concatenate(
        [
            w_router,
            ln1_gain[:, None],
            ln2_gain[:, None],
            jnp.zeros((rows, side_width - groups - 2), bf16),
        ],
        axis=1,
    )
    dense = gather_rows(jnp.concatenate([w_qkv, w_out, side], axis=1), "dp", me_o)
    first = gather_rows(expert_in[0], "dp", me_o)
    second = gather_rows(expert_out[0], "dp", me_o)
    bias = lax.all_gather(expert_bias, "dp", axis=1, tiled=True)

    routes = [expert_index, expert_slot, route_kept]
    dense_width = dense.shape[1]
    state = []
    boxes = []
    for m in range(MB):
        shared = [tokens] + routes + [cotangent]
        shared_specs = [of_batch(a.shape, m) for a in shared]
        outs = call(
            functools.partial(forward_kernel, groups, capacity),
            "forward",
            [SCALAR] + shared_specs + [whole(dense.shape)],
            [
                like((SEQ, 3 * D), bf16),
                like((HEADS, SEQ, SEQ), bf16),
                like((SEQ, D), bf16),
                like((SEQ, D), f32),
                like((SEQ, groups), f32),
            ]
            + [like((2 * capacity, D), bf16)] * groups,
            [me_e] + shared + [dense],
            2 * SEQ * D * (4 * D + 3 * slots) + 4 * SEQ * SEQ * D,
        )
        state.append(outs[:5])
        sends = outs[5:]
        boxes.append(
            [sends[0]]
            + [lax.ppermute(sends[k], "expert", xor_pairs(groups, k)) for k in range(1, groups)]
        )

    actives, hiddens, returned = [], [], []
    for m in range(MB):
        args = list(boxes[m]) + [first, bias, second]
        outs = call(
            functools.partial(expert_kernel, groups, capacity),
            "experts",
            [whole(a.shape) for a in args],
            [like((2 * capacity, D), bf16)] * groups + [like((slots, wide), bf16)] * 2,
            args,
            8 * slots * D * wide,
        )
        actives.append(outs[groups])
        hiddens.append(outs[groups + 1])
        returned.append(
            [outs[0]]
            + [lax.ppermute(outs[k], "expert", xor_pairs(groups, k)) for k in range(1, groups)]
        )
    all_boxes = [box for m in range(MB) for box in boxes[m]]
    args = all_boxes + actives
    second_parts = call(
        functools.partial(second_grad_kernel, groups, capacity, owners),
        "second_grad",
        [whole(a.shape) for a in args],
        [like((owners, expert_out.shape[1], D), bf16)],
        args,
        2 * MB * slots * D * wide,
    )[0]
    args = all_boxes + hiddens
    first_parts = call(
        functools.partial(first_grad_kernel, groups, capacity, owners),
        "first_grad",
        [whole(a.shape) for a in args],
        [like((owners, expert_in.shape[1] + 8, wide), bf16)],
        args,
        2 * MB * slots * D * wide,
    )[0]
    d_second = scatter_sum(second_parts, "dp", me_owner)
    d_first = scatter_sum(first_parts, "dp", me_owner)

    outputs, token_grads = [], []
    total = None
    for m in range(MB):
        shared = [tokens] + routes + [cotangent]
        shared_specs = [of_batch(a.shape, m) for a in shared]
        rest = [dense] + list(state[m]) + list(returned[m]) + ([] if m == 0 else [total])
        outs = call(
            functools.partial(backward_kernel, groups, capacity, m > 0),
            "backward",
            [SCALAR] + shared_specs + [whole(a.shape) for a in rest],
            [
                like((1, SEQ, D), bf16),
                like((1, SEQ, D), f32),
                like((D, dense_width), f32),
            ],
            [me_e] + shared + rest,
            2 * SEQ * D * (8 * D + 3 * slots) + 8 * SEQ * SEQ * D,
        )
        outputs.append(outs[0])
        token_grads.append(outs[1])
        total = outs[2]
    low = total.astype(bf16)
    for k in (1 << b for b in range((groups - 1).bit_length())):
        low = (low.astype(f32) + lax.ppermute(low, "expert", xor_pairs(groups, k)).astype(f32)).astype(bf16)
    d_dense = scatter_sum(low.reshape(owners, rows, dense_width), "dp", me_owner)
    columns = expert_bias.shape[1]
    own_rows = expert_in.shape[1]
    d_bias = lax.dynamic_slice_in_dim(d_first[own_rows], me_owner * columns, columns, 0)
    return (
        jnp.stack(outputs, axis=0),
        jnp.stack(token_grads, axis=0),
        d_dense[:, 4 * D + groups],
        d_dense[:, : 3 * D],
        d_dense[:, 3 * D : 4 * D],
        d_dense[:, 4 * D + groups + 1],
        d_dense[:, 4 * D : 4 * D + groups],
        d_first[:own_rows][None],
        d_bias[None],
        d_second[None],
    )


def solution(mesh):
    images = P(None, ("dp", "expert"), None, None)
    weights = (
        P("dp"),
        P("dp", None),
        P("dp", None),
        P("dp"),
        P("dp", None),
        P("expert", "dp", None),
        P("expert", "dp"),
        P("expert", "dp", None),
    )
    return jax.shard_map(
        body,
        mesh=mesh,
        in_specs=(images,) * 4 + weights + (images,),
        out_specs=(images, images) + weights,
        check_vma=False,
    )
```

time: 872 us -> 351 us (0.40)
  the two profiles are of different devices: /device:TPU:0 before, /device:TPU:8 now
where the time goes in v1:
time: 351 us; the launch traced here: 346 us
  waiting for transfers between devices  114 us (32%)
  starting transfers between devices  85.2 us (24%)
  Pallas kernels  62.7 us (18%)
  local copies, waits for them, and re-layouts  52.5 us (15%)
  blocking collectives  16.7 us (5%)
  other arithmetic  12.8 us (4%)
    ppermute x21, waiting for transfers between devices, scatter_sum(): total += lax.ppermute(sent, axis, xor_pairs(count, k)).astype(f32)  83.9 us
    pallas_call x14, Pallas kernels, call(): pl.pallas_call(kernel, grid=grid, in_specs=in_specs, out_specs=[whole(o.s...  62.7 us
    ppermute x21, starting transfers between devices, scatter_sum(): total += lax.ppermute(sent, axis, xor_pairs(count, k)).astype(f32)  40.4 us
    unnamed x186, local copies, waits for them, and re-layouts  38.7 us
    ppermute x21, starting transfers between devices, gather_rows(): lax.ppermute(piece, axis, xor_pairs(count, k))  31.6 us
    ppermute x21, waiting for transfers between devices, gather_rows(): lax.ppermute(piece, axis, xor_pairs(count, k))  28.7 us
    unnamed x1, blocking collectives  16.7 us
  transfers between devices with their start and end apart: 62, of which 19 were waited for; matrix products, arithmetic and copies ran while one was open for 7% of the time, Pallas kernels for 16%

profile of v1, /device:TPU:8, one launch (start us, length us, event | category | flops | bytes accessed | tf_op | source)
XLA Modules:
  0.0 345.9 jit_solution(14373180176856191875)
XLA Ops:
  3.7 4.3 %collective-permute-start.14 = (bf16[48,1536]{1,0:T(8,128)(2,1)}, bf16[48,1536]{1,0:T(8,128)(2,1)S(1)}, u32[]{:S(2)}, u32[]{:S(2)}) collective-permute-start(bf16[48,1536]{1,0:T(8,128)(2,1)} %bitcast.89), channel_id=1, source_target_pairs={{0,20},{4,16},{8,28},{12,24},{16,4},{20,0},{24,12},{28,8},{1,21},{... | collective-permute-start | bytes 442376 | tf_op jit(solution)/shard_map/ppermute | solution.py:313
  9.8 11.8 %collective-permute-done.16.refs_7_ = bf16[48,1536]{1,0:T(8,128)(2,1)S(1)} collective-permute-done((bf16[48,1536]{1,0:T(8,128)(2,1)}, bf16[48,1536]{1,0:T(8,128)(2,1)S(1)}, u32[]{:S(2)}, u32[]{:S(2)}) %collective-permute-start.16) | collective-permute-done | bytes 147488 | tf_op jit(solution)/shard_map/ppermute | solution.py:313
  29.7 10.6 %collective-permute-done.13.refs_4_ = bf16[48,1536]{1,0:T(8,128)(2,1)S(1)} collective-permute-done((bf16[48,1536]{1,0:T(8,128)(2,1)}, bf16[48,1536]{1,0:T(8,128)(2,1)S(1)}, u32[]{:S(2)}, u32[]{:S(2)}) %collective-permute-start.13) | collective-permute-done | bytes 147488 | tf_op jit(solution)/shard_map/ppermute | solution.py:313
  41.9 4.4 %collective-permute-start.4 = (bf16[48,1664]{1,0:T(8,128)(2,1)S(1)}, bf16[48,1664]{1,0:T(8,128)(2,1)S(1)}, u32[]{:S(2)}, u32[]{:S(2)}) collective-permute-start(bf16[48,1664]{1,0:T(8,128)(2,1)S(1)} %concatenate.3.refs_0_), channel_id=1, source_target_pairs={{0,20},{4,16},{8,28},{12,24},{16,4},{20,0},{24,12},{28,8},{1,21},{... | collective-permute-start | bytes 479240 | tf_op jit(solution)/shard_map/ppermute | solution.py:313
  81.1 4.2 %forward.3 = (bf16[197,1152]{1,0:T(8,128)(2,1)S(1)}, bf16[6,197,197]{2,1,0:T(8,128)(2,1)S(1)}, bf16[197,384]{1,0:T(8,128)(2,1)S(1)}, f32[197,384]{1,0:T(8,128)S(...) custom-call(s32[1]{0:T(128)} %bitcast.me_ref, ...), custom_call_target="tpu_custom_call" | custom-call | flops 524391936 | bytes 4362984 | tf_op jit(solution)/shard_map/forward/pallas_call | solution.py:294
  92.3 16.7 %all-reduce = bf16[1536]{0:T(1024)(128)(2,1)S(1)} all-reduce(bf16[1536]{0:T(1024)(128)(2,1)S(1)} %dynamic-update-slice), channel_id=1, replica_groups=mesh['dp'=8,'expert'=4] {'dp'}, use_global_device_ids=true, to_apply=%add | all-reduce | flops 1536 | bytes 6144
  128.3 6.0 %experts.3 = (bf16[256,384]{1,0:T(8,128)(2,1)S(1)}, bf16[256,384]{1,0:T(8,128)(2,1)S(1)}, bf16[256,384]{1,0:T(8,128)(2,1)S(1)}, bf16[256,384]{1,0:T(8,128)(2,1)S...) custom-call(bf16[256,384]{1,0:T(8,128)(2,1)S(1)} %get-tuple-element.69.refs_0_, ...), custom_call_target="tpu_custom_call" | custom-call | flops 2415919104 | bytes 7080960 | tf_op jit(solution)/shard_map/experts/pallas_call | solution.py:294
  138.1 5.3 %experts.4 = (bf16[256,384]{1,0:T(8,128)(2,1)S(1)}, bf16[256,384]{1,0:T(8,128)(2,1)S(1)}, bf16[256,384]{1,0:T(8,128)(2,1)S(1)}, bf16[256,384]{1,0:T(8,128)(2,1)S...) custom-call(bf16[256,384]{1,0:T(8,128)(2,1)S(1)} %get-tuple-element.83.refs_0_.refs_4_, ...), custom_call_target="tpu_custom_call" | custom-call | flops 2415919104 | bytes 7080960 | tf_op jit(solution)/shard_map/experts/pallas_call | solution.py:294
  147.6 4.6 %experts.5 = (bf16[256,384]{1,0:T(8,128)(2,1)S(1)}, bf16[256,384]{1,0:T(8,128)(2,1)}, bf16[256,384]{1,0:T(8,128)(2,1)S(1)}, bf16[256,384]{1,0:T(8,128)(2,1)S(1)}...) custom-call(bf16[256,384]{1,0:T(8,128)(2,1)S(1)} %get-tuple-element.98.refs_0_.refs_8_, ...), custom_call_target="tpu_custom_call" | custom-call | flops 2415919104 | bytes 7080960 | tf_op jit(solution)/shard_map/experts/pallas_call | solution.py:294
  155.5 7.1 %backward.3 = (bf16[1,197,384]{2,1,0:T(8,128)(2,1)S(1)}, f32[1,197,384]{2,1,0:T(8,128)S(1)}, f32[384,1664]{1,0:T(8,128)}) custom-call(s32[1]{0:T(128)} %bitcast.me_ref, bf16[3,1,197,384]{3,2,1,0:T(8,128)(2,1)S(1)} %copy-done, s32[3,1,197,2]{3,2,1,0:T(8,128)S(1)} %copy.29.index_ref, s32[3,1,197,2]{3,2,1,0:T(8,128)S(1)} %copy.30.slot_ref, ...), custom_call_target="tpu_custom_call" | custom-call | flops 816393216 | bytes 7372776 | tf_op jit(solution)/shard_map/backward/pallas_call | solution.py:294
  162.6 9.2 %backward.4 = (bf16[1,197,384]{2,1,0:T(8,128)(2,1)S(1)}, f32[1,197,384]{2,1,0:T(8,128)S(1)}, f32[384,1664]{1,0:T(8,128)}) custom-call(s32[1]{0:T(128)} %bitcast.me_ref, bf16[3,1,197,384]{3,2,1,0:T(8,128)(2,1)S(1)} %copy-done, s32[3,1,197,2]{3,2,1,0:T(8,128)S(1)} %copy.29.index_ref, s32[3,1,197,2]{3,2,1,0:T(8,128)S(1)} %copy.30.slot_ref, ...), custom_call_target="tpu_custom_call" | custom-call | flops 816393216 | bytes 9928680 | tf_op jit(solution)/shard_map/backward/pallas_call | solution.py:294
  171.8 8.8 %backward.5 = (bf16[1,197,384]{2,1,0:T(8,128)(2,1)S(1)}, f32[1,197,384]{2,1,0:T(8,128)S(1)}, f32[384,1664]{1,0:T(8,128)}) custom-call(s32[1]{0:T(128)} %bitcast.me_ref, bf16[3,1,197,384]{3,2,1,0:T(8,128)(2,1)S(1)} %copy-done, s32[3,1,197,2]{3,2,1,0:T(8,128)S(1)} %copy.29.index_ref, s32[3,1,197,2]{3,2,1,0:T(8,128)S(1)} %copy.30.slot_ref, ...), custom_call_target="tpu_custom_call" | custom-call | flops 816393216 | bytes 9928680 | tf_op jit(solution)/shard_map/backward/pallas_call | solution.py:294
  186.1 4.8 %second_grad.1 = bf16[8,192,384]{2,1,0:T(8,128)(2,1)S(1)} custom-call(bf16[256,384]{1,0:T(8,128)(2,1)S(1)} %get-tuple-element.69.refs_0_, bf16[256,384]{1,0:T(8,128)(2,1)S(1)} %collective-permute-done.7.refs_1_, bf16[256,384]{1,0:T(8,128)(2,1)} %collective-permute-done.8.refs_2_, bf16[256,384]{1,0:T(8,128)(2,1)} %collective-permute-done.9.refs_3_, ...), custom_call_target="tpu_custom_call" | custom-call | flops 1811939328 | bytes 8257536 | tf_op jit(solution)/shard_map/second_grad/pallas_call | solution.py:294
  195.3 3.7 %collective-permute-start.59 = (bf16[192,384]{1,0:T(8,128)(2,1)S(1)}, bf16[192,384]{1,0:T(8,128)(2,1)S(1)}, u32[]{:S(2)}, u32[]{:S(2)}) collective-permute-start(bf16[192,384]{1,0:T(8,128)(2,1)S(1)} %get-tuple-element.146), channel_id=1, source_target_pairs={{0,20},{4,16},{8,28},{12,24},{16,4},{20,0},{24,12},{28,8},{1,21},{... | collective-permute-start | bytes 442376 | tf_op jit(solution)/shard_map/ppermute | solution.py:331
  202.3 4.2 %first_grad.1 = bf16[8,56,1536]{2,1,0:T(8,128)(2,1)S(1)} custom-call(bf16[256,384]{1,0:T(8,128)(2,1)S(1)} %get-tuple-element.69.refs_0_, bf16[256,384]{1,0:T(8,128)(2,1)S(1)} %collective-permute-done.7.refs_1_, bf16[256,384]{1,0:T(8,128)(2,1)} %collective-permute-done.8.refs_2_, bf16[256,384]{1,0:T(8,128)(2,1)} %collective-permute-done.9.refs_3_, ...), custom_call_target="tpu_custom_call" | custom-call | flops 1811939328 | bytes 8454144 | tf_op jit(solution)/shard_map/first_grad/pallas_call | solution.py:294
  218.1 3.6 %collective-permute-start.53 = (bf16[56,1536]{1,0:T(8,128)(2,1)}, bf16[56,1536]{1,0:T(8,128)(2,1)S(1)}, u32[]{:S(2)}, u32[]{:S(2)}) collective-permute-start(bf16[56,1536]{1,0:T(8,128)(2,1)} %get-tuple-element.130), channel_id=1, source_target_pairs={{0,24},{4,28},{8,16},{12,20},{16,8},{20,12},{24,0},{28,4},{1,25},{... | collective-permute-start | bytes 516104 | tf_op jit(solution)/shard_map/ppermute | solution.py:331
  225.9 6.3 %collective-permute-done.56 = bf16[192,384]{1,0:T(8,128)(2,1)} collective-permute-done((bf16[192,384]{1,0:T(8,128)(2,1)}, bf16[192,384]{1,0:T(8,128)(2,1)}, u32[]{:S(2)}, u32[]{:S(2)}) %collective-permute-start.56) | collective-permute-done | bytes 147488 | tf_op jit(solution)/shard_map/ppermute | solution.py:331
  238.5 4.9 %collective-permute-done.53 = bf16[56,1536]{1,0:T(8,128)(2,1)S(1)} collective-permute-done((bf16[56,1536]{1,0:T(8,128)(2,1)}, bf16[56,1536]{1,0:T(8,128)(2,1)S(1)}, u32[]{:S(2)}, u32[]{:S(2)}) %collective-permute-start.53) | collective-permute-done | bytes 172064 | tf_op jit(solution)/shard_map/ppermute | solution.py:331
  270.3 4.3 %collective-permute-done.42 = bf16[48,1664]{0,1:T(8,128)(2,1)S(1)} collective-permute-done((bf16[48,1664]{0,1:T(8,128)(2,1)}, bf16[48,1664]{0,1:T(8,128)(2,1)S(1)}, u32[]{:S(2)}, u32[]{:S(2)}) %collective-permute-start.42) | collective-permute-done | bytes 159776 | tf_op jit(solution)/shard_map/ppermute | solution.py:331
  274.6 6.7 %collective-permute-start.47 = (bf16[48,1664]{0,1:T(8,128)(2,1)}, bf16[48,1664]{0,1:T(8,128)(2,1)}, u32[]{:S(2)}, u32[]{:S(2)}) collective-permute-start(bf16[48,1664]{0,1:T(8,128)(2,1)} %bitcast.96), channel_id=1, source_target_pairs={{0,28},{4,24},{8,20},{12,16},{16,12},{20,8},{24,4},{28,0},{1,29},{... | collective-permute-start | bytes 479240 | tf_op jit(solution)/shard_map/ppermute | solution.py:331
  284.4 30.5 %collective-permute-done.44 = bf16[48,1664]{0,1:T(8,128)(2,1)S(1)} collective-permute-done((bf16[48,1664]{0,1:T(8,128)(2,1)}, bf16[48,1664]{0,1:T(8,128)(2,1)S(1)}, u32[]{:S(2)}, u32[]{:S(2)}) %collective-permute-start.44) | collective-permute-done | bytes 159776 | tf_op jit(solution)/shard_map/ppermute | solution.py:331
  314.9 9.1 %collective-permute-done.45 = bf16[48,1664]{0,1:T(8,128)(2,1)S(1)} collective-permute-done((bf16[48,1664]{0,1:T(8,128)(2,1)}, bf16[48,1664]{0,1:T(8,128)(2,1)S(1)}, u32[]{:S(2)}, u32[]{:S(2)}) %collective-permute-start.45) | collective-permute-done | bytes 159776 | tf_op jit(solution)/shard_map/ppermute | solution.py:331
  324.0 12.0 %collective-permute-done.46 = bf16[48,1664]{0,1:T(8,128)(2,1)} collective-permute-done((bf16[48,1664]{0,1:T(8,128)(2,1)}, bf16[48,1664]{0,1:T(8,128)(2,1)}, u32[]{:S(2)}, u32[]{:S(2)}) %collective-permute-start.46) | collective-permute-done | bytes 159776 | tf_op jit(solution)/shard_map/ppermute | solution.py:331
  336.1 5.2 %collective-permute-done.47 = bf16[48,1664]{0,1:T(8,128)(2,1)} collective-permute-done((bf16[48,1664]{0,1:T(8,128)(2,1)}, bf16[48,1664]{0,1:T(8,128)(2,1)}, u32[]{:S(2)}, u32[]{:S(2)}) %collective-permute-start.47) | collective-permute-done | bytes 159776 | tf_op jit(solution)/shard_map/ppermute | solution.py:331
  (331 shorter events, 155.4 us)
Async XLA Ops:
  3.2 22.3 %collective-permute-start.15 = (bf16[48,1536]{1,0:T(8,128)(2,1)}, bf16[48,1536]{1,0:T(8,128)(2,1)S(1)}, u32[]{:S(2)}, u32[]{:S(2)}) collective-permute-start(bf16[48,1536]{1,0:T(8,128)(2,1)} %bitcast.88), channel_id=1, source_target_pairs={{0,24},{4,28},{8,16},{12,20},{16,8},{20,12},{24,0},{28,4},{1,25},{... | collective-permute-start | bytes 442376 | tf_op jit(solution)/shard_map/ppermute | solution.py:313
  3.7 24.7 %collective-permute-start.14 = (bf16[48,1536]{1,0:T(8,128)(2,1)}, bf16[48,1536]{1,0:T(8,128)(2,1)S(1)}, u32[]{:S(2)}, u32[]{:S(2)}) collective-permute-start(bf16[48,1536]{1,0:T(8,128)(2,1)} %bitcast.89), channel_id=1, source_target_pairs={{0,20},{4,16},{8,28},{12,24},{16,4},{20,0},{24,12},{28,8},{1,21},{... | collective-permute-start | bytes 442376 | tf_op jit(solution)/shard_map/ppermute | solution.py:313
  8.0 32.2 %collective-permute-start.13 = (bf16[48,1536]{1,0:T(8,128)(2,1)}, bf16[48,1536]{1,0:T(8,128)(2,1)S(1)}, u32[]{:S(2)}, u32[]{:S(2)}) collective-permute-start(bf16[48,1536]{1,0:T(8,128)(2,1)} %bitcast.90), channel_id=1, source_target_pairs={{0,16},{4,20},{8,24},{12,28},{16,0},{20,4},{24,8},{28,12},{1,17},{... | collective-permute-start | bytes 442376 | tf_op jit(solution)/shard_map/ppermute | solution.py:313
  8.1 33.2 %collective-permute-start.12 = (bf16[48,1536]{1,0:T(8,128)(2,1)}, bf16[48,1536]{1,0:T(8,128)(2,1)S(1)}, u32[]{:S(2)}, u32[]{:S(2)}) collective-permute-start(bf16[48,1536]{1,0:T(8,128)(2,1)} %bitcast.91), channel_id=1, source_target_pairs={{0,12},{4,8},{8,4},{12,0},{16,28},{20,24},{24,20},{28,16},{1,13},{... | collective-permute-start | bytes 442376 | tf_op jit(solution)/shard_map/ppermute | solution.py:313
  22.2 24.1 %collective-permute-start.11 = (bf16[48,1536]{1,0:T(8,128)(2,1)}, bf16[48,1536]{1,0:T(8,128)(2,1)S(1)}, u32[]{:S(2)}, u32[]{:S(2)}) collective-permute-start(bf16[48,1536]{1,0:T(8,128)(2,1)} %bitcast.92), channel_id=1, source_target_pairs={{0,8},{4,12},{8,0},{12,4},{16,24},{20,28},{24,16},{28,20},{1,9},{5... | collective-permute-start | bytes 442376 | tf_op jit(solution)/shard_map/ppermute | solution.py:313
  26.2 21.5 %collective-permute-start.6 = (bf16[48,1664]{1,0:T(8,128)(2,1)S(1)}, bf16[48,1664]{1,0:T(8,128)(2,1)S(1)}, u32[]{:S(2)}, u32[]{:S(2)}) collective-permute-start(bf16[48,1664]{1,0:T(8,128)(2,1)S(1)} %concatenate.3.refs_0_), channel_id=1, source_target_pairs={{0,28},{4,24},{8,20},{12,16},{16,12},{20,8},{24,4},{28,0},{1,29},{... | collective-permute-start | bytes 479240 | tf_op jit(solution)/shard_map/ppermute | solution.py:313
  29.0 22.4 %collective-permute-start.5 = (bf16[48,1664]{1,0:T(8,128)(2,1)S(1)}, bf16[48,1664]{1,0:T(8,128)(2,1)S(1)}, u32[]{:S(2)}, u32[]{:S(2)}) collective-permute-start(bf16[48,1664]{1,0:T(8,128)(2,1)S(1)} %concatenate.3.refs_0_), channel_id=1, source_target_pairs={{0,24},{4,28},{8,16},{12,20},{16,8},{20,12},{24,0},{28,4},{1,25},{... | collective-permute-start | bytes 479240 | tf_op jit(solution)/shard_map/ppermute | solution.py:313
  55.6 22.4 %collective-permute-start.23 = (bf16[192,384]{1,0:T(8,128)(2,1)}, bf16[192,384]{1,0:T(8,128)(2,1)}, u32[]{:S(2)}, u32[]{:S(2)}) collective-permute-start(bf16[192,384]{1,0:T(8,128)(2,1)} %bitcast.8.refs_0_), channel_id=1, source_target_pairs={{0,28},{4,24},{8,20},{12,16},{16,12},{20,8},{24,4},{28,0},{1,29},{... | collective-permute-start | bytes 442376 | tf_op jit(solution)/shard_map/ppermute | solution.py:313
  60.8 28.1 %collective-permute-start.21 = (bf16[192,384]{1,0:T(8,128)(2,1)}, bf16[192,384]{1,0:T(8,128)(2,1)}, u32[]{:S(2)}, u32[]{:S(2)}) collective-permute-start(bf16[192,384]{1,0:T(8,128)(2,1)} %bitcast.8.refs_0_), channel_id=1, source_target_pairs={{0,20},{4,16},{8,28},{12,24},{16,4},{20,0},{24,12},{28,8},{1,21},{... | collective-permute-start | bytes 442376 | tf_op jit(solution)/shard_map/ppermute | solution.py:313
  65.0 23.9 %collective-permute-start.20 = (bf16[192,384]{1,0:T(8,128)(2,1)}, bf16[192,384]{1,0:T(8,128)(2,1)}, u32[]{:S(2)}, u32[]{:S(2)}) collective-permute-start(bf16[192,384]{1,0:T(8,128)(2,1)} %bitcast.8.refs_0_), channel_id=1, source_target_pairs={{0,16},{4,20},{8,24},{12,28},{16,0},{20,4},{24,8},{28,12},{1,17},{... | collective-permute-start | bytes 442376 | tf_op jit(solution)/shard_map/ppermute | solution.py:313
  78.0 38.4 %collective-permute-start.18 = (bf16[192,384]{1,0:T(8,128)(2,1)}, bf16[192,384]{1,0:T(8,128)(2,1)}, u32[]{:S(2)}, u32[]{:S(2)}) collective-permute-start(bf16[192,384]{1,0:T(8,128)(2,1)} %bitcast.8.refs_0_), channel_id=1, source_target_pairs={{0,8},{4,12},{8,0},{12,4},{16,24},{20,28},{24,16},{28,20},{1,9},{5... | collective-permute-start | bytes 442376 | tf_op jit(solution)/shard_map/ppermute | solution.py:313
  79.7 36.7 %collective-permute-start.17 = (bf16[192,384]{1,0:T(8,128)(2,1)}, bf16[192,384]{1,0:T(8,128)(2,1)}, u32[]{:S(2)}, u32[]{:S(2)}) collective-permute-start(bf16[192,384]{1,0:T(8,128)(2,1)} %bitcast.8.refs_0_), channel_id=1, source_target_pairs={{0,4},{4,0},{8,12},{12,8},{16,20},{20,16},{24,28},{28,24},{1,5},{5... | collective-permute-start | bytes 442376 | tf_op jit(solution)/shard_map/ppermute | solution.py:313
  88.9 37.5 %collective-permute-start.7 = (bf16[256,384]{1,0:T(8,128)(2,1)}, bf16[256,384]{1,0:T(8,128)(2,1)S(1)}, u32[]{:S(2)}, u32[]{:S(2)}) collective-permute-start(bf16[256,384]{1,0:T(8,128)(2,1)} %get-tuple-element.70), channel_id=1, source_target_pairs={{0,1},{1,0},{2,3},{3,2},{4,5},{5,4},{6,7},{7,6},{8,9},{9,8},{10,11... | collective-permute-start | bytes 589832 | tf_op jit(solution)/shard_map/ppermute | solution.py:401
  88.9 37.7 %collective-permute-start.8 = (bf16[256,384]{1,0:T(8,128)(2,1)}, bf16[256,384]{1,0:T(8,128)(2,1)}, u32[]{:S(2)}, u32[]{:S(2)}) collective-permute-start(bf16[256,384]{1,0:T(8,128)(2,1)} %get-tuple-element.71), channel_id=1, source_target_pairs={{0,2},{1,3},{2,0},{3,1},{4,6},{5,7},{6,4},{7,5},{8,10},{9,11},{10,... | collective-permute-start | bytes 589832 | tf_op jit(solution)/shard_map/ppermute | solution.py:401
  90.5 36.7 %collective-permute-start.9 = (bf16[256,384]{1,0:T(8,128)(2,1)}, bf16[256,384]{1,0:T(8,128)(2,1)}, u32[]{:S(2)}, u32[]{:S(2)}) collective-permute-start(bf16[256,384]{1,0:T(8,128)(2,1)} %get-tuple-element.72), channel_id=1, source_target_pairs={{0,3},{1,2},{2,1},{3,0},{4,7},{5,6},{6,5},{7,4},{8,11},{9,10},{10,... | collective-permute-start | bytes 589832 | tf_op jit(solution)/shard_map/ppermute | solution.py:401
  121.3 23.3 %collective-permute-start.33 = (bf16[256,384]{1,0:T(8,128)(2,1)S(1)}, bf16[256,384]{1,0:T(8,128)(2,1)S(1)}, u32[]{:S(2)}, u32[]{:S(2)}) collective-permute-start(bf16[256,384]{1,0:T(8,128)(2,1)S(1)} %get-tuple-element.99), channel_id=1, source_target_pairs={{0,1},{1,0},{2,3},{3,2},{4,5},{5,4},{6,7},{7,6},{8,9},{9,8},{10,11... | collective-permute-start | bytes 589832 | tf_op jit(solution)/shard_map/ppermute | solution.py:401
  121.4 24.3 %collective-permute-start.34 = (bf16[256,384]{1,0:T(8,128)(2,1)S(1)}, bf16[256,384]{1,0:T(8,128)(2,1)S(1)}, u32[]{:S(2)}, u32[]{:S(2)}) collective-permute-start(bf16[256,384]{1,0:T(8,128)(2,1)S(1)} %get-tuple-element.100), channel_id=1, source_target_pairs={{0,2},{1,3},{2,0},{3,1},{4,6},{5,7},{6,4},{7,5},{8,10},{9,11},{10,... | collective-permute-start | bytes 589832 | tf_op jit(solution)/shard_map/ppermute | solution.py:401
  192.3 23.5 %collective-permute-start.60 = (bf16[192,384]{1,0:T(8,128)(2,1)S(1)}, bf16[192,384]{1,0:T(8,128)(2,1)S(1)}, u32[]{:S(2)}, u32[]{:S(2)}) collective-permute-start(bf16[192,384]{1,0:T(8,128)(2,1)S(1)} %get-tuple-element.145), channel_id=1, source_target_pairs={{0,24},{4,28},{8,16},{12,20},{16,8},{20,12},{24,0},{28,4},{1,25},{... | collective-permute-start | bytes 442376 | tf_op jit(solution)/shard_map/ppermute | solution.py:331
  201.7 50.7 %collective-permute-start.40 = (bf16[384,1664]{1,0:T(8,128)(2,1)}, bf16[384,1664]{1,0:T(8,128)(2,1)}, u32[]{:S(2)}, u32[]{:S(2)}) collective-permute-start(bf16[384,1664]{1,0:T(8,128)(2,1)} %add_convert_fusion.1), channel_id=1, source_target_pairs={{0,2},{1,3},{2,0},{3,1},{4,6},{5,7},{6,4},{7,5},{8,10},{9,11},{10,... | collective-permute-start | bytes 3833864 | tf_op jit(solution)/shard_map/ppermute | solution.py:466
  218.1 25.3 %collective-permute-start.53 = (bf16[56,1536]{1,0:T(8,128)(2,1)}, bf16[56,1536]{1,0:T(8,128)(2,1)S(1)}, u32[]{:S(2)}, u32[]{:S(2)}) collective-permute-start(bf16[56,1536]{1,0:T(8,128)(2,1)} %get-tuple-element.130), channel_id=1, source_target_pairs={{0,24},{4,28},{8,16},{12,20},{16,8},{20,12},{24,0},{28,4},{1,25},{... | collective-permute-start | bytes 516104 | tf_op jit(solution)/shard_map/ppermute | solution.py:331
  266.8 48.1 %collective-permute-start.44 = (bf16[48,1664]{0,1:T(8,128)(2,1)}, bf16[48,1664]{0,1:T(8,128)(2,1)S(1)}, u32[]{:S(2)}, u32[]{:S(2)}) collective-permute-start(bf16[48,1664]{0,1:T(8,128)(2,1)} %bitcast.21), channel_id=1, source_target_pairs={{0,16},{4,20},{8,24},{12,28},{16,0},{20,4},{24,8},{28,12},{1,17},{... | collective-permute-start | bytes 479240 | tf_op jit(solution)/shard_map/ppermute | solution.py:331
  267.8 56.2 %collective-permute-start.45 = (bf16[48,1664]{0,1:T(8,128)(2,1)}, bf16[48,1664]{0,1:T(8,128)(2,1)S(1)}, u32[]{:S(2)}, u32[]{:S(2)}) collective-permute-start(bf16[48,1664]{0,1:T(8,128)(2,1)} %bitcast.98), channel_id=1, source_target_pairs={{0,20},{4,16},{8,28},{12,24},{16,4},{20,0},{24,12},{28,8},{1,21},{... | collective-permute-start | bytes 479240 | tf_op jit(solution)/shard_map/ppermute | solution.py:331
  269.7 66.4 %collective-permute-start.46 = (bf16[48,1664]{0,1:T(8,128)(2,1)}, bf16[48,1664]{0,1:T(8,128)(2,1)}, u32[]{:S(2)}, u32[]{:S(2)}) collective-permute-start(bf16[48,1664]{0,1:T(8,128)(2,1)} %bitcast.97), channel_id=1, source_target_pairs={{0,24},{4,28},{8,16},{12,20},{16,8},{20,12},{24,0},{28,4},{1,25},{... | collective-permute-start | bytes 479240 | tf_op jit(solution)/shard_map/ppermute | solution.py:331
  274.6 66.7 %collective-permute-start.47 = (bf16[48,1664]{0,1:T(8,128)(2,1)}, bf16[48,1664]{0,1:T(8,128)(2,1)}, u32[]{:S(2)}, u32[]{:S(2)}) collective-permute-start(bf16[48,1664]{0,1:T(8,128)(2,1)} %bitcast.96), channel_id=1, source_target_pairs={{0,28},{4,24},{8,20},{12,16},{16,12},{20,8},{24,4},{28,0},{1,29},{... | collective-permute-start | bytes 479240 | tf_op jit(solution)/shard_map/ppermute | solution.py:331
  (125 other events, 986.8 us)

commit v2 on v1

--- a/solution.py
+++ b/solution.py
@@ -146,53 +146,73 @@
         backs[g][capacity:] = grad_inbox[g * capacity : (g + 1) * capacity]
 
 
-def second_grad_kernel(groups, capacity, owners, *refs):
+def place(keep_ref, send_ref, at, value):
+    @pl.when((at & 1) == 0)
+    def _():
+        keep_ref[at >> 1] = value
+
+    @pl.when((at & 1) == 1)
+    def _():
+        send_ref[at >> 1] = value
+
+
+def second_grad_kernel(groups, capacity, owners, me_ref, *refs):
     boxes = [refs[m * groups : (m + 1) * groups] for m in range(MB)]
     actives = refs[MB * groups : MB * groups + MB]
-    out_ref = refs[-1]
-    rows = out_ref.shape[1]
+    keep_ref, send_ref = refs[-2:]
+    rows = keep_ref.shape[1]
     grads = [
         jnp.concatenate([box[capacity:] for box in boxes[m]], axis=0) for m in range(MB)
     ]
     wide = owners * rows
-    step = wide // 3 if (wide // 3) % rows == 0 else wide // 2
+    step = wide // 2
     for at in range(0, wide, step):
         total = dot(actives[0][:, at : at + step], grads[0], 0, 0)
         for m in range(1, MB):
             total += dot(actives[m][:, at : at + step], grads[m], 0, 0)
-        total = total.astype(bf16)
         for j in range(step // rows):
-            out_ref[at // rows + j] = total[j * rows : (j + 1) * rows]
-
-
-def first_grad_kernel(groups, capacity, owners, *refs):
+            part = total[j * rows : (j + 1) * rows].astype(bf16)
+            place(keep_ref, send_ref, (at // rows + j) ^ me_ref[1], part)
+
+
+def first_grad_kernel(groups, capacity, owners, me_ref, *refs):
     boxes = [refs[m * groups : (m + 1) * groups] for m in range(MB)]
     hiddens = refs[MB * groups : MB * groups + MB]
-    out_ref = refs[-1]
+    keep_ref, send_ref = refs[-2:]
     rows = D // owners
-    extra = out_ref.shape[1] - rows
+    extra = keep_ref.shape[1] - rows
     inboxes = [
         jnp.concatenate([box[:capacity] for box in boxes[m]], axis=0) for m in range(MB)
     ]
-    wide = out_ref.shape[2]
+    wide = keep_ref.shape[2]
     step = wide // 3
+    totals, biases = [], []
     for at in range(0, wide, step):
         total = dot(inboxes[0], hiddens[0][:, at : at + step], 0, 0)
         bias = jnp.sum(hiddens[0][:, at : at + step].astype(f32), axis=0, keepdims=True)
         for m in range(1, MB):
             total += dot(inboxes[m], hiddens[m][:, at : at + step], 0, 0)
             bias += jnp.sum(hiddens[m][:, at : at + step].astype(f32), axis=0, keepdims=True)
-        total = total.astype(bf16)
-        bias = jnp.broadcast_to(bias, (extra, step)).astype(bf16)
-        for j in range(owners):
-            out_ref[j, :rows, at : at + step] = total[j * rows : (j + 1) * rows]
-            out_ref[j, rows:, at : at + step] = bias
-
-
-def backward_kernel(groups, capacity, has_total, me_ref, tokens_ref, index_ref, slot_ref, kept_ref, cot_ref, dense_ref, packed_ref, attn_ref, attended_ref, middle_ref, router_ref, *refs):
+        totals.append(total)
+        biases.append(jnp.broadcast_to(bias, (extra, step)))
+    for j in range(owners):
+        part = jnp.concatenate(
+            [
+                jnp.concatenate([total[j * rows : (j + 1) * rows], bias], axis=0)
+                for total, bias in zip(totals, biases)
+            ],
+            axis=1,
+        )
+        place(keep_ref, send_ref, j ^ me_ref[1], part.astype(bf16))
+
+
+def backward_kernel(groups, capacity, has_total, last, me_ref, tokens_ref, index_ref, slot_ref, kept_ref, cot_ref, dense_ref, packed_ref, attn_ref, attended_ref, middle_ref, router_ref, *refs):
     backs = refs[:groups]
     total_ref = refs[groups] if has_total else None
-    output_ref, d_tokens_ref, grads_ref = refs[-3:]
+    if last:
+        output_ref, d_tokens_ref, keep_ref, send_ref = refs[-4:]
+    else:
+        output_ref, d_tokens_ref, grads_ref = refs[-3:]
     me = me_ref[0]
     side = side_rows(dense_ref)
     gain_one = side[groups : groups + 1]
@@ -258,17 +278,143 @@
     packed_grad = dot((hat * gain_one).astype(bf16), grad_packed, 0, 0)
     side_grad += dot(grad_normed * hat, column_one, 0, 0, precision=HIGHEST)
     d_tokens_ref[0] = grad_middle + norm_back(grad_normed * gain_one, hat, rate)
+    pieces = []
     for lo, part in ((0, packed_grad), (3 * D, out_grad), (4 * D, side_grad)):
         hi = lo + part.shape[1]
         if has_total:
             part = part + total_ref[:, lo:hi]
-        grads_ref[:, lo:hi] = part
+        pieces.append(part)
+        if not last:
+            grads_ref[:, lo:hi] = part
+    if last:
+        joined = jnp.concatenate(pieces, axis=1).astype(bf16)
+        left, right = split_halves(joined)
+        core = me & 1
+        rows = keep_ref.shape[1]
+        for j in range(keep_ref.shape[0]):
+            at = j ^ me_ref[1]
+            cut = slice(j * rows, (j + 1) * rows)
+
+            @pl.when(core == 0)
+            def _(at=at, cut=cut):
+                keep_ref[at] = left[cut]
+                send_ref[at] = right[cut]
+
+            @pl.when(core == 1)
+            def _(at=at, cut=cut):
+                keep_ref[at] = right[cut]
+                send_ref[at] = left[cut]
+
+
+def split_halves(joined):
+    half = half_width(joined.shape[1])
+    return joined[:, :half], joined[:, joined.shape[1] - half :]
+
+
+def half_width(width):
+    return -(-width // (2 * LANES)) * LANES
+
+
+def join_halves(left, right, width):
+    half = left.shape[1]
+    return jnp.concatenate([left, right[:, 2 * half - width :]], axis=1)
+
+
+def pack_kernel(me_ref, qkv_ref, out_ref, side_ref, first_ref, second_ref, bias_ref, half_ref, pack_ref):
+    joined = jnp.concatenate([qkv_ref[...], out_ref[...], side_ref[...]], axis=1)
+    left, right = split_halves(joined)
+
+    @pl.when((me_ref[0] & 1) == 0)
+    def _():
+        half_ref[...] = left
+
+    @pl.when((me_ref[0] & 1) == 1)
+    def _():
+        half_ref[...] = right
+
+    rows = first_ref.shape[1]
+    tall = second_ref.shape[1]
+    pack_ref[:tall] = second_ref[0]
+    for c in range(first_ref.shape[2] // D):
+        pack_ref[tall + c * rows : tall + (c + 1) * rows] = first_ref[0, :, c * D : (c + 1) * D]
+    pack_ref[2 * tall :] = bias_ref[...]
 
 
 def arrange_kernel(count, me_ref, *refs):
     out_ref = refs[-1]
     for k in range(count):
-        out_ref[me_ref[0] ^ k] = refs[k][...]
+        out_ref[me_ref[1] ^ k] = refs[k][...]
+
+
+def join_kernel(me_ref, mine_ref, other_ref, out_ref):
+    width = out_ref.shape[1]
+
+    @pl.when((me_ref[0] & 1) == 0)
+    def _():
+        out_ref[...] = join_halves(mine_ref[...], other_ref[...], width)
+
+    @pl.when((me_ref[0] & 1) == 1)
+    def _():
+        out_ref[...] = join_halves(other_ref[...], mine_ref[...], width)
+
+
+def unpack_kernel(count, me_ref, *refs):
+    first_ref, second_ref, bias_ref, table = refs[count:]
+    rows = first_ref.shape[1]
+    tall = second_ref.shape[1]
+    for k in range(count):
+        at = me_ref[1] ^ k
+        second_ref[at] = refs[k][:tall]
+        for c in range(first_ref.shape[2] // D):
+            first_ref[at, :, c * D : (c + 1) * D] = refs[k][tall + c * rows : tall + (c + 1) * rows]
+        table[at] = refs[k][2 * tall :]
+    fold = D // tall
+    for i in range(count // fold):
+        line = table[fold * i][:1].astype(f32)
+        for r in range(1, fold):
+            line += table[fold * i + r][r : r + 1].astype(f32)
+        bias_ref[:, i * D : (i + 1) * D] = line
+
+
+def merge_kernel(keep_ref, got_ref, own_ref, *sends):
+    for k in range(keep_ref.shape[0]):
+        total = keep_ref[k].astype(f32) + got_ref[k].astype(f32)
+        if k == 0:
+            own_ref[...] = total
+        else:
+            sends[k - 1][...] = total.astype(bf16)
+
+
+def deal_kernel(keep_ref, got_ref, own_ref, send_ref):
+    for k in range(keep_ref.shape[0]):
+        total = (keep_ref[k].astype(f32) + got_ref[k].astype(f32)).astype(bf16)
+        if k % 2 == 0:
+            own_ref[k // 2] = total
+        else:
+            send_ref[k // 2] = total
+
+
+def total_kernel(own_ref, *refs):
+    total = own_ref[...].astype(f32)
+    for ref in refs[:-1]:
+        total += ref[...].astype(f32)
+    refs[-1][...] = total.astype(refs[-1].dtype)
+
+
+def finish_kernel(me_ref, mine_ref, other_ref, qkv_ref, out_ref, side_ref):
+    def write(left, right):
+        joined = join_halves(left, right, 4 * D + LANES).astype(f32)
+        qkv_ref[...] = joined[:, : 3 * D]
+        out_ref[...] = joined[:, 3 * D : 4 * D]
+        side_ref[...] = joined[:, 4 * D :]
+
+    @pl.when((me_ref[0] & 1) == 0)
+    def _():
+        write(mine_ref[...], other_ref[...])
+
+    @pl.when((me_ref[0] & 1) == 1)
+    def _():
+        write(other_ref[...], mine_ref[...])
 
 
 def params():
@@ -288,17 +434,20 @@
 SCALAR = pl.BlockSpec(memory_space=pltpu.SMEM)
 
 
-def call(kernel, name, in_specs, outs, args, flops, grid=(1,)):
+def call(kernel, name, outs, args, us, in_specs=None, scratch=()):
+    if in_specs is None:
+        in_specs = [SCALAR if a.dtype == jnp.int32 else whole(a.shape) for a in args]
     moved = sum(a.size * a.dtype.itemsize for a in args)
     moved += sum(a.size * a.dtype.itemsize for a in outs)
     return pl.pallas_call(
         kernel,
-        grid=grid,
+        grid=(1,),
         in_specs=in_specs,
         out_specs=[whole(o.shape) for o in outs],
         out_shape=outs,
+        scratch_shapes=list(scratch),
         compiler_params=params(),
-        cost_estimate=pl.CostEstimate(flops=flops, bytes_accessed=moved, transcendentals=0),
+        cost_estimate=pl.CostEstimate(flops=int(us * 1e9), bytes_accessed=moved, transcendentals=0),
         name=name,
     )(*args)
 
@@ -307,29 +456,32 @@
     return jax.ShapeDtypeStruct(tuple(shape), dtype)
 
 
-def gather_rows(piece, axis, me):
+def send(value, axis, k):
+    return lax.ppermute(value, axis, xor_pairs(lax.axis_size(axis), k))
+
+
+def gather_pieces(own, axis):
     count = lax.axis_size(axis)
-    pieces = [piece] + [
-        lax.ppermute(piece, axis, xor_pairs(count, k)) for k in range(1, count)
-    ]
-    out = call(
-        functools.partial(arrange_kernel, count),
-        "arrange",
-        [SCALAR] + [whole(piece.shape)] * count,
-        [like((count,) + piece.shape, piece.dtype)],
-        [me] + pieces,
-        0,
-    )[0]
-    return out.reshape((count * piece.shape[0],) + piece.shape[1:])
-
-
-def scatter_sum(parts, axis, me):
-    count = lax.axis_size(axis)
-    total = lax.dynamic_index_in_dim(parts, me, 0, keepdims=False).astype(f32)
-    for k in range(1, count):
-        sent = lax.dynamic_index_in_dim(parts, me ^ k, 0, keepdims=False)
-        total += lax.ppermute(sent, axis, xor_pairs(count, k)).astype(f32)
-    return total
+    pieces = [own] + [None] * (count - 1)
+    order = sorted(range(2, count, 2), reverse=True)
+    for k in order:
+        pieces[k] = send(own, axis, k)
+    for k in [0] + order:
+        pieces[k + 1] = send(pieces[k], axis, 1)
+    return pieces
+
+
+def sum_rest(keep, got, axis):
+    shape = keep.shape[1:]
+    count = keep.shape[0]
+    merged = call(
+        merge_kernel,
+        "merge",
+        [like(shape, f32)] + [like(shape, bf16)] * (count - 1),
+        [keep, got],
+        2,
+    )
+    return [merged[0]] + [send(merged[k], axis, 2 * k) for k in reversed(range(1, count))]
 
 
 def body(
@@ -352,37 +504,66 @@
     capacity = 8 * (5 * SEQ // (16 * groups) + 1)
     slots = groups * capacity
     wide = expert_in.shape[2]
-    me_expert = lax.axis_index("expert")
-    me_owner = lax.axis_index("dp")
-    me_e = me_expert.reshape(1).astype(jnp.int32)
-    me_o = me_owner.reshape(1).astype(jnp.int32)
-    side_width = LANES
     rows = w_qkv.shape[0]
+    tall = expert_out.shape[1]
+    dense_width = 4 * D + LANES
+    half = half_width(dense_width)
+    me = jnp.stack([lax.axis_index("expert"), lax.axis_index("dp")]).astype(jnp.int32)
     side = jnp.concatenate(
         [
             w_router,
             ln1_gain[:, None],
             ln2_gain[:, None],
-            jnp.zeros((rows, side_width - groups - 2), bf16),
+            jnp.zeros((rows, LANES - groups - 2), bf16),
         ],
         axis=1,
     )
-    dense = gather_rows(jnp.concatenate([w_qkv, w_out, side], axis=1), "dp", me_o)
-    first = gather_rows(expert_in[0], "dp", me_o)
-    second = gather_rows(expert_out[0], "dp", me_o)
-    bias = lax.all_gather(expert_bias, "dp", axis=1, tiled=True)
+    fold = D // tall
+    bias_rows = jnp.pad(
+        (jnp.eye(fold, dtype=bf16)[:, :, None] * expert_bias[0]).reshape(fold, D),
+        ((0, 16 - fold), (0, 0)),
+    )
+    own_half, own_pack = call(
+        pack_kernel,
+        "pack",
+        [like((rows, half), bf16), like((2 * tall + 16, D), bf16)],
+        [me, w_qkv, w_out, side, expert_in, expert_out, bias_rows],
+        2,
+    )
+    halves = gather_pieces(own_half, "dp")
+    mine = call(
+        functools.partial(arrange_kernel, owners),
+        "arrange",
+        [like((owners, rows, half), bf16)],
+        [me] + halves,
+        2,
+    )[0].reshape(D, half)
+    other = send(mine, "expert", 1)
+    dense = call(join_kernel, "join", [like((D, dense_width), bf16)], [me, mine, other], 2)[0]
+    packs = gather_pieces(own_pack, "dp")
+    first, second, bias = call(
+        functools.partial(unpack_kernel, owners),
+        "unpack",
+        [
+            like((owners, rows, wide), bf16),
+            like((owners, tall, D), bf16),
+            like((1, wide), f32),
+        ],
+        [me] + packs,
+        4,
+        scratch=[pltpu.VMEM((owners, 16, D), bf16)],
+    )
+    first = first.reshape(D, wide)
+    second = second.reshape(wide, D)
 
     routes = [expert_index, expert_slot, route_kept]
-    dense_width = dense.shape[1]
     state = []
     boxes = []
     for m in range(MB):
         shared = [tokens] + routes + [cotangent]
-        shared_specs = [of_batch(a.shape, m) for a in shared]
         outs = call(
             functools.partial(forward_kernel, groups, capacity),
             "forward",
-            [SCALAR] + shared_specs + [whole(dense.shape)],
             [
                 like((SEQ, 3 * D), bf16),
                 like((HEADS, SEQ, SEQ), bf16),
@@ -391,92 +572,113 @@
                 like((SEQ, groups), f32),
             ]
             + [like((2 * capacity, D), bf16)] * groups,
-            [me_e] + shared + [dense],
-            2 * SEQ * D * (4 * D + 3 * slots) + 4 * SEQ * SEQ * D,
+            [me] + shared + [dense],
+            4,
+            in_specs=[SCALAR] + [of_batch(a.shape, m) for a in shared] + [whole(dense.shape)],
         )
         state.append(outs[:5])
         sends = outs[5:]
         boxes.append(
-            [sends[0]]
-            + [lax.ppermute(sends[k], "expert", xor_pairs(groups, k)) for k in range(1, groups)]
+            [sends[0]] + [send(sends[k], "expert", k) for k in reversed(range(1, groups))][::-1]
         )
 
     actives, hiddens, returned = [], [], []
     for m in range(MB):
-        args = list(boxes[m]) + [first, bias, second]
         outs = call(
             functools.partial(expert_kernel, groups, capacity),
             "experts",
-            [whole(a.shape) for a in args],
             [like((2 * capacity, D), bf16)] * groups + [like((slots, wide), bf16)] * 2,
-            args,
-            8 * slots * D * wide,
+            list(boxes[m]) + [first, bias, second],
+            5,
         )
         actives.append(outs[groups])
         hiddens.append(outs[groups + 1])
         returned.append(
-            [outs[0]]
-            + [lax.ppermute(outs[k], "expert", xor_pairs(groups, k)) for k in range(1, groups)]
+            [outs[0]] + [send(outs[k], "expert", k) for k in reversed(range(1, groups))][::-1]
         )
     all_boxes = [box for m in range(MB) for box in boxes[m]]
-    args = all_boxes + actives
-    second_parts = call(
+    second_keep, second_send = call(
         functools.partial(second_grad_kernel, groups, capacity, owners),
         "second_grad",
-        [whole(a.shape) for a in args],
-        [like((owners, expert_out.shape[1], D), bf16)],
-        args,
-        2 * MB * slots * D * wide,
-    )[0]
-    args = all_boxes + hiddens
-    first_parts = call(
+        [like((owners // 2, tall, D), bf16)] * 2,
+        [me] + all_boxes + actives,
+        5,
+    )
+    first_keep, first_send = call(
         functools.partial(first_grad_kernel, groups, capacity, owners),
         "first_grad",
-        [whole(a.shape) for a in args],
-        [like((owners, expert_in.shape[1] + 8, wide), bf16)],
-        args,
-        2 * MB * slots * D * wide,
-    )[0]
-    d_second = scatter_sum(second_parts, "dp", me_owner)
-    d_first = scatter_sum(first_parts, "dp", me_owner)
+        [like((owners // 2, rows + 8, wide), bf16)] * 2,
+        [me] + all_boxes + hiddens,
+        5,
+    )
+    dense_late, second_send, first_send = lax.optimization_barrier(
+        (dense, second_send, first_send)
+    )
+    second_terms = sum_rest(second_keep, send(second_send, "dp", 1), "dp")
+    first_terms = sum_rest(first_keep, send(first_send, "dp", 1), "dp")
 
     outputs, token_grads = [], []
     total = None
     for m in range(MB):
+        last = m == MB - 1
         shared = [tokens] + routes + [cotangent]
-        shared_specs = [of_batch(a.shape, m) for a in shared]
-        rest = [dense] + list(state[m]) + list(returned[m]) + ([] if m == 0 else [total])
+        rest = [dense_late] + list(state[m]) + list(returned[m]) + ([] if m == 0 else [total])
         outs = call(
-            functools.partial(backward_kernel, groups, capacity, m > 0),
+            functools.partial(backward_kernel, groups, capacity, m > 0, last),
             "backward",
-            [SCALAR] + shared_specs + [whole(a.shape) for a in rest],
-            [
-                like((1, SEQ, D), bf16),
-                like((1, SEQ, D), f32),
-                like((D, dense_width), f32),
-            ],
-            [me_e] + shared + rest,
-            2 * SEQ * D * (8 * D + 3 * slots) + 8 * SEQ * SEQ * D,
+            [like((1, SEQ, D), bf16), like((1, SEQ, D), f32)]
+            + (
+                [like((owners, rows, half), bf16)] * 2
+                if last
+                else [like((D, dense_width), f32)]
+            ),
+            [me] + shared + rest,
+            8,
+            in_specs=[SCALAR]
+            + [of_batch(a.shape, m) for a in shared]
+            + [whole(a.shape) for a in rest],
         )
         outputs.append(outs[0])
         token_grads.append(outs[1])
         total = outs[2]
-    low = total.astype(bf16)
-    for k in (1 << b for b in range((groups - 1).bit_length())):
-        low = (low.astype(f32) + lax.ppermute(low, "expert", xor_pairs(groups, k)).astype(f32)).astype(bf16)
-    d_dense = scatter_sum(low.reshape(owners, rows, dense_width), "dp", me_owner)
-    columns = expert_bias.shape[1]
-    own_rows = expert_in.shape[1]
-    d_bias = lax.dynamic_slice_in_dim(d_first[own_rows], me_owner * columns, columns, 0)
+        dense_send = outs[-1]
+    keep, share = call(
+        deal_kernel,
+        "deal",
+        [like((owners // 2, rows, half), bf16)] * 2,
+        [total, send(dense_send, "expert", 1)],
+        2,
+    )
+    dense_terms = sum_rest(keep, send(share, "dp", 1), "dp")
+    reduced = call(total_kernel, "total", [like((rows, half), bf16)], dense_terms, 1)[0]
+    bits = [1 << b for b in range(1, (groups - 1).bit_length())]
+    for k in bits:
+        reduced = call(
+            total_kernel,
+            "total",
+            [like((rows, half), bf16)],
+            [reduced, send(reduced, "expert", k)],
+            1,
+        )[0]
+    d_qkv, d_out, d_side = call(
+        finish_kernel,
+        "finish",
+        [like((rows, 3 * D), f32), like((rows, D), f32), like((rows, LANES), f32)],
+        [me, reduced, send(reduced, "expert", 1)],
+        1,
+    )
+    d_second = call(total_kernel, "total", [like((tall, D), f32)], second_terms, 1)[0]
+    d_first = call(total_kernel, "total", [like((rows + 8, wide), f32)], first_terms, 1)[0]
+    d_bias = lax.dynamic_slice_in_dim(d_first[rows], me[1] * tall, tall, 0)
     return (
         jnp.stack(outputs, axis=0),
         jnp.stack(token_grads, axis=0),
-        d_dense[:, 4 * D + groups],
-        d_dense[:, : 3 * D],
-        d_dense[:, 3 * D : 4 * D],
-        d_dense[:, 4 * D + groups + 1],
-        d_dense[:, 4 * D : 4 * D + groups],
-        d_first[:own_rows][None],
+        d_side[:, groups],
+        d_qkv,
+        d_out,
+        d_side[:, groups + 1],
+        d_side[:, :groups],
+        d_first[:rows][None],
         d_bias[None],
         d_second[None],
     )

time: 351 us -> 234 us (0.67)
  the two profiles are of different devices: /device:TPU:8 before, /device:TPU:0 now
where the time goes in v2:
time: 234 us; the launch traced here: 232 us
  waiting for transfers between devices  74.3 us (32%)
  Pallas kernels  71 us (30%)
  starting transfers between devices  57.1 us (24%)
  local copies, waits for them, and re-layouts  25.9 us (11%)
    ppermute x48, waiting for transfers between devices, send(): return lax.ppermute(value, axis, xor_pairs(lax.axis_size(axis), k))  74.3 us
    pallas_call x24, Pallas kernels, call(): pl.pallas_call(kernel, grid=(1,), in_specs=in_specs, out_specs=[whole(o.s...  71 us
    ppermute x48, starting transfers between devices, send(): return lax.ppermute(value, axis, xor_pairs(lax.axis_size(axis), k))  57.1 us
    unnamed x108, local copies, waits for them, and re-layouts  21.9 us
  transfers between devices with their start and end apart: 48, of which 19 were waited for; matrix products, arithmetic and copies ran while one was open for 2% of the time, Pallas kernels for 22%

profile of v2, /device:TPU:0, one launch (start us, length us, event | category | flops | bytes accessed | tf_op | source)
XLA Modules:
  0.0 231.5 jit_solution(8668400646827225810)
XLA Ops:
  8.3 5.1 %collective-permute-start.5 = (bf16[48,896]{1,0:T(8,128)(2,1)S(1)}, bf16[48,896]{1,0:T(8,128)(2,1)S(1)}, u32[]{:S(2)}, u32[]{:S(2)}) collective-permute-start(bf16[48,896]{1,0:T(8,128)(2,1)S(1)} %get-tuple-element.94.refs_0_), channel_id=1, source_target_pairs={{0,24},{4,28},{8,16},{12,20},{16,8},{20,12},{24,0},{28,4},{1,25},{... | collective-permute-start | bytes 258056 | tf_op jit(solution)/shard_map/ppermute | solution.py:460
  18.3 3.8 %collective-permute-start.22 = (bf16[400,384]{1,0:T(8,128)(2,1)S(1)}, bf16[400,384]{1,0:T(8,128)(2,1)S(1)}, u32[]{:S(2)}, u32[]{:S(2)}) collective-permute-start(bf16[400,384]{1,0:T(8,128)(2,1)S(1)} %get-tuple-element.107.refs_0_), channel_id=1, source_target_pairs={{0,24},{4,28},{8,16},{12,20},{16,8},{20,12},{24,0},{28,4},{1,25},{... | collective-permute-start | bytes 921608 | tf_op jit(solution)/shard_map/ppermute | solution.py:460
  22.1 10.3 %collective-permute-done.3.refs_4_ = bf16[48,896]{1,0:T(8,128)(2,1)S(1)} collective-permute-done((bf16[48,896]{1,0:T(8,128)(2,1)S(1)}, bf16[48,896]{1,0:T(8,128)(2,1)S(1)}, u32[]{:S(2)}, u32[]{:S(2)}) %collective-permute-start.3) | collective-permute-done | bytes 86048 | tf_op jit(solution)/shard_map/ppermute | solution.py:460
  32.4 3.7 %collective-permute-start.4 = (bf16[48,896]{1,0:T(8,128)(2,1)S(1)}, bf16[48,896]{1,0:T(8,128)(2,1)S(1)}, u32[]{:S(2)}, u32[]{:S(2)}) collective-permute-start(bf16[48,896]{1,0:T(8,128)(2,1)S(1)} %collective-permute-done.3.refs_4_), channel_id=1, source_target_pairs={{0,4},{4,0},{8,12},{12,8},{16,20},{20,16},{24,28},{28,24},{1,5},{5... | collective-permute-start | bytes 258056 | tf_op jit(solution)/shard_map/ppermute | solution.py:460
  43.4 3.5 %collective-permute-done.20.refs_4_ = bf16[400,384]{1,0:T(8,128)(2,1)S(1)} collective-permute-done((bf16[400,384]{1,0:T(8,128)(2,1)S(1)}, bf16[400,384]{1,0:T(8,128)(2,1)S(1)}, u32[]{:S(2)}, u32[]{:S(2)}) %collective-permute-start.20) | collective-permute-done | bytes 307232 | tf_op jit(solution)/shard_map/ppermute | solution.py:460
  51.6 6.6 %collective-permute-done.23.refs_7_ = bf16[400,384]{1,0:T(8,128)(2,1)} collective-permute-done((bf16[400,384]{1,0:T(8,128)(2,1)S(1)}, bf16[400,384]{1,0:T(8,128)(2,1)}, u32[]{:S(2)}, u32[]{:S(2)}) %collective-permute-start.23) | collective-permute-done | bytes 307232 | tf_op jit(solution)/shard_map/ppermute | solution.py:460
  58.2 6.6 %collective-permute-done.21.refs_5_ = bf16[400,384]{1,0:T(8,128)(2,1)} collective-permute-done((bf16[400,384]{1,0:T(8,128)(2,1)S(1)}, bf16[400,384]{1,0:T(8,128)(2,1)}, u32[]{:S(2)}, u32[]{:S(2)}) %collective-permute-start.21) | collective-permute-done | bytes 307232 | tf_op jit(solution)/shard_map/ppermute | solution.py:460
  64.8 6.1 %collective-permute-done.19.refs_3_ = bf16[400,384]{1,0:T(8,128)(2,1)} collective-permute-done((bf16[400,384]{1,0:T(8,128)(2,1)}, bf16[400,384]{1,0:T(8,128)(2,1)}, u32[]{:S(2)}, u32[]{:S(2)}) %collective-permute-start.19) | collective-permute-done | bytes 307232 | tf_op jit(solution)/shard_map/ppermute | solution.py:460
  73.6 4.0 %forward.5 = (bf16[197,1152]{1,0:T(8,128)(2,1)S(1)}, bf16[6,197,197]{2,1,0:T(8,128)(2,1)S(1)}, bf16[197,384]{1,0:T(8,128)(2,1)S(1)}, f32[197,384]{1,0:T(8,128)S(...) custom-call(s32[2]{0:T(128)S(1)} %pad_add_fusion.me_ref, ...), custom_call_target="tpu_custom_call" | custom-call | flops 4000000000 | bytes 4362988 | tf_op jit(solution)/shard_map/forward/pallas_call | solution.py:442
  79.2 4.0 %forward.3 = (bf16[197,1152]{1,0:T(8,128)(2,1)S(1)}, bf16[6,197,197]{2,1,0:T(8,128)(2,1)S(1)}, bf16[197,384]{1,0:T(8,128)(2,1)S(1)}, f32[197,384]{1,0:T(8,128)S(...) custom-call(s32[2]{0:T(128)S(1)} %pad_add_fusion.me_ref, ...), custom_call_target="tpu_custom_call" | custom-call | flops 4000000000 | bytes 4362988 | tf_op jit(solution)/shard_map/forward/pallas_call | solution.py:442
  89.6 4.0 %forward.4 = (bf16[197,1152]{1,0:T(8,128)(2,1)S(1)}, bf16[6,197,197]{2,1,0:T(8,128)(2,1)S(1)}, bf16[197,384]{1,0:T(8,128)(2,1)S(1)}, f32[197,384]{1,0:T(8,128)S(...) custom-call(s32[2]{0:T(128)S(1)} %pad_add_fusion.me_ref, ...), custom_call_target="tpu_custom_call" | custom-call | flops 4000000000 | bytes 4362988 | tf_op jit(solution)/shard_map/forward/pallas_call | solution.py:442
  103.3 4.9 %experts.3 = (bf16[256,384]{1,0:T(8,128)(2,1)S(1)}, bf16[256,384]{1,0:T(8,128)(2,1)S(1)}, bf16[256,384]{1,0:T(8,128)(2,1)S(1)}, bf16[256,384]{1,0:T(8,128)(2,1)S...) custom-call(bf16[256,384]{1,0:T(8,128)(2,1)S(1)} %get-tuple-element.95.refs_0_, ...), custom_call_target="tpu_custom_call" | custom-call | flops 5000000000 | bytes 7084032 | tf_op jit(solution)/shard_map/experts/pallas_call | solution.py:442
  111.5 5.0 %experts.4 = (bf16[256,384]{1,0:T(8,128)(2,1)S(1)}, bf16[256,384]{1,0:T(8,128)(2,1)S(1)}, bf16[256,384]{1,0:T(8,128)(2,1)S(1)}, bf16[256,384]{1,0:T(8,128)(2,1)S...) custom-call(bf16[256,384]{1,0:T(8,128)(2,1)S(1)} %get-tuple-element.99.refs_0_.refs_4_, ...), custom_call_target="tpu_custom_call" | custom-call | flops 5000000000 | bytes 7084032 | tf_op jit(solution)/shard_map/experts/pallas_call | solution.py:442
  120.5 4.9 %experts.5 = (bf16[256,384]{1,0:T(8,128)(2,1)S(1)}, bf16[256,384]{1,0:T(8,128)(2,1)S(1)}, bf16[256,384]{1,0:T(8,128)(2,1)S(1)}, bf16[256,384]{1,0:T(8,128)(2,1)S...) custom-call(bf16[256,384]{1,0:T(8,128)(2,1)S(1)} %get-tuple-element.103.refs_0_.refs_8_, ...), custom_call_target="tpu_custom_call" | custom-call | flops 5000000000 | bytes 7084032 | tf_op jit(solution)/shard_map/experts/pallas_call | solution.py:442
  128.0 4.3 %first_grad.1 = (bf16[4,56,1536]{2,1,0:T(8,128)(2,1)S(1)}, bf16[4,56,1536]{2,1,0:T(8,128)(2,1)S(1)}) custom-call(s32[2]{0:T(128)S(1)} %pad_add_fusion.me_ref, bf16[256,384]{1,0:T(8,128)(2,1)S(1)} %get-tuple-element.95.refs_0_, bf16[256,384]{1,0:T(8,128)(2,1)S(1)} %collective-permute-done.8.refs_1_, bf16[256,384]{1,0:T(8,128)(2,1)S(1)} %collective-permute-done.9.refs_2_, ...), custom_call_target="tpu_custom_call" | custom-call | flops 5000000000 | bytes 8454152 | tf_op jit(solution)/shard_map/first_grad/pallas_call | solution.py:442
  133.2 6.3 %second_grad.1 = (bf16[4,192,384]{2,1,0:T(8,128)(2,1)S(1)}, bf16[4,192,384]{2,1,0:T(8,128)(2,1)}) custom-call(s32[2]{0:T(128)S(1)} %pad_add_fusion.me_ref, bf16[256,384]{1,0:T(8,128)(2,1)S(1)} %get-tuple-element.95.refs_0_, bf16[256,384]{1,0:T(8,128)(2,1)S(1)} %collective-permute-done.8.refs_1_, bf16[256,384]{1,0:T(8,128)(2,1)S(1)} %collective-permute-done.9.refs_2_, ...), custom_call_target="tpu_custom_call" | custom-call | flops 5000000000 | bytes 8257544 | tf_op jit(solution)/shard_map/second_grad/pallas_call | solution.py:442
  141.8 7.6 %backward.3 = (bf16[1,197,384]{2,1,0:T(8,128)(2,1)S(1)}, f32[1,197,384]{2,1,0:T(8,128)S(1)}, f32[384,1664]{1,0:T(8,128)}) custom-call(s32[2]{0:T(128)S(1)} %pad_add_fusion.me_ref, bf16[3,1,197,384]{3,2,1,0:T(8,128)(2,1)S(1)} %copy-done.1, s32[3,1,197,2]{3,2,1,0:T(8,128)S(1)} %copy.58.index_ref, s32[3,1,197,2]{3,2,1,0:T(8,128)S(1)} %copy.59.slot_ref, ...), custom_call_target="tpu_custom_call" | custom-call | flops 8000000000 | bytes 7372780 | tf_op jit(solution)/shard_map/backward/pallas_call | solution.py:442
  149.5 8.7 %backward.4 = (bf16[1,197,384]{2,1,0:T(8,128)(2,1)S(1)}, f32[1,197,384]{2,1,0:T(8,128)S(1)}, f32[384,1664]{1,0:T(8,128)}) custom-call(s32[2]{0:T(128)S(1)} %pad_add_fusion.me_ref, bf16[3,1,197,384]{3,2,1,0:T(8,128)(2,1)S(1)} %copy-done.1, s32[3,1,197,2]{3,2,1,0:T(8,128)S(1)} %copy.58.index_ref, s32[3,1,197,2]{3,2,1,0:T(8,128)S(1)} %copy.59.slot_ref, ...), custom_call_target="tpu_custom_call" | custom-call | flops 8000000000 | bytes 9928684 | tf_op jit(solution)/shard_map/backward/pallas_call | solution.py:442
  158.3 8.7 %backward.5 = (bf16[1,197,384]{2,1,0:T(8,128)(2,1)S(1)}, f32[1,197,384]{2,1,0:T(8,128)S(1)}, bf16[8,48,896]{2,1,0:T(8,128)(2,1)S(1)}, bf16[8,48,896]{2,1,0:T(8,128)(2,1)}) custom-call(s32[2]{0:T(128)S(1)} %pad_add_fusion.me_ref, bf16[3,1,197,384]{3,2,1,0:T(8,128)(2,1)S(1)} %copy-done.1, s32[3,1,197,2]{3,2,1,0:T(8,128)S(1)} %copy.58.index_ref, ...), custom_call_target="tpu_custom_call" | custom-call | flops 8000000000 | bytes 8749036 | tf_op jit(solution)/shard_map/backward/pallas_call | solution.py:442
  175.6 9.4 %collective-permute-done.44.got_ref = bf16[4,192,384]{2,1,0:T(8,128)(2,1)} collective-permute-done((bf16[4,192,384]{2,1,0:T(8,128)(2,1)}, bf16[4,192,384]{2,1,0:T(8,128)(2,1)}, u32[]{:S(2)}, u32[]{:S(2)}) %collective-permute-start.44) | collective-permute-done | bytes 589856 | tf_op jit(solution)/shard_map/ppermute | solution.py:460
  187.9 2.8 %collective-permute-start.47 = (bf16[192,384]{1,0:T(8,128)(2,1)S(1)}, bf16[192,384]{1,0:T(8,128)(2,1)S(1)}, u32[]{:S(2)}, u32[]{:S(2)}) collective-permute-start(bf16[192,384]{1,0:T(8,128)(2,1)S(1)} %get-tuple-element.177), channel_id=1, source_target_pairs={{0,8},{4,12},{8,0},{12,4},{16,24},{20,28},{24,16},{28,20},{1,9},{5... | collective-permute-start | bytes 442376 | tf_op jit(solution)/shard_map/ppermute | solution.py:460
  190.7 8.9 %collective-permute-done.40.got_ref = bf16[4,56,1536]{2,1,0:T(8,128)(2,1)S(1)} collective-permute-done((bf16[4,56,1536]{2,1,0:T(8,128)(2,1)S(1)}, bf16[4,56,1536]{2,1,0:T(8,128)(2,1)S(1)}, u32[]{:S(2)}, u32[]{:S(2)}) %collective-permute-start.40) | collective-permute-done | bytes 688160 | tf_op jit(solution)/shard_map/ppermute | solution.py:460
  209.0 6.9 %collective-permute-start.37 = (bf16[48,896]{1,0:T(8,128)(2,1)S(1)}, bf16[48,896]{1,0:T(8,128)(2,1)S(1)}, u32[]{:S(2)}, u32[]{:S(2)}) collective-permute-start(bf16[48,896]{1,0:T(8,128)(2,1)S(1)} %get-tuple-element.162), channel_id=1, source_target_pairs={{0,8},{4,12},{8,0},{12,4},{16,24},{20,28},{24,16},{28,20},{1,9},{5... | collective-permute-start | bytes 258056 | tf_op jit(solution)/shard_map/ppermute | solution.py:460
  215.9 5.0 %collective-permute-done.42.refs_1_ = bf16[56,1536]{1,0:T(8,128)(2,1)S(1)} collective-permute-done((bf16[56,1536]{1,0:T(8,128)(2,1)S(1)}, bf16[56,1536]{1,0:T(8,128)(2,1)S(1)}, u32[]{:S(2)}, u32[]{:S(2)}) %collective-permute-start.42) | collective-permute-done | bytes 172064 | tf_op jit(solution)/shard_map/ppermute | solution.py:460
  (225 shorter events, 88.9 us)
Async XLA Ops:
  13.4 19.0 %collective-permute-start.3 = (bf16[48,896]{1,0:T(8,128)(2,1)S(1)}, bf16[48,896]{1,0:T(8,128)(2,1)S(1)}, u32[]{:S(2)}, u32[]{:S(2)}) collective-permute-start(bf16[48,896]{1,0:T(8,128)(2,1)S(1)} %get-tuple-element.94.refs_0_), channel_id=1, source_target_pairs={{0,16},{4,20},{8,24},{12,28},{16,0},{20,4},{24,8},{28,12},{1,17},{... | collective-permute-start | bytes 258056 | tf_op jit(solution)/shard_map/ppermute | solution.py:460
  13.4 19.0 %collective-permute-start.1 = (bf16[48,896]{1,0:T(8,128)(2,1)S(1)}, bf16[48,896]{1,0:T(8,128)(2,1)S(1)}, u32[]{:S(2)}, u32[]{:S(2)}) collective-permute-start(bf16[48,896]{1,0:T(8,128)(2,1)S(1)} %get-tuple-element.94.refs_0_), channel_id=1, source_target_pairs={{0,8},{4,12},{8,0},{12,4},{16,24},{20,28},{24,16},{28,20},{1,9},{5... | collective-permute-start | bytes 258056 | tf_op jit(solution)/shard_map/ppermute | solution.py:460
  14.0 18.4 %collective-permute-start = (bf16[48,896]{1,0:T(8,128)(2,1)S(1)}, bf16[48,896]{1,0:T(8,128)(2,1)S(1)}, u32[]{:S(2)}, u32[]{:S(2)}) collective-permute-start(bf16[48,896]{1,0:T(8,128)(2,1)S(1)} %get-tuple-element.94.refs_0_), channel_id=1, source_target_pairs={{0,4},{4,0},{8,12},{12,8},{16,20},{20,16},{24,28},{28,24},{1,5},{5... | collective-permute-start | bytes 258056 | tf_op jit(solution)/shard_map/ppermute | solution.py:460
  16.6 19.6 %collective-permute-start.6 = (bf16[48,896]{1,0:T(8,128)(2,1)S(1)}, bf16[48,896]{1,0:T(8,128)(2,1)S(1)}, u32[]{:S(2)}, u32[]{:S(2)}) collective-permute-start(bf16[48,896]{1,0:T(8,128)(2,1)S(1)} %collective-permute-done.5.refs_6_), channel_id=1, source_target_pairs={{0,4},{4,0},{8,12},{12,8},{16,20},{20,16},{24,28},{28,24},{1,5},{5... | collective-permute-start | bytes 258056 | tf_op jit(solution)/shard_map/ppermute | solution.py:460
  18.3 24.0 %collective-permute-start.22 = (bf16[400,384]{1,0:T(8,128)(2,1)S(1)}, bf16[400,384]{1,0:T(8,128)(2,1)S(1)}, u32[]{:S(2)}, u32[]{:S(2)}) collective-permute-start(bf16[400,384]{1,0:T(8,128)(2,1)S(1)} %get-tuple-element.107.refs_0_), channel_id=1, source_target_pairs={{0,24},{4,28},{8,16},{12,20},{16,8},{20,12},{24,0},{28,4},{1,25},{... | collective-permute-start | bytes 921608 | tf_op jit(solution)/shard_map/ppermute | solution.py:460
  32.4 16.0 %collective-permute-start.18 = (bf16[400,384]{1,0:T(8,128)(2,1)S(1)}, bf16[400,384]{1,0:T(8,128)(2,1)}, u32[]{:S(2)}, u32[]{:S(2)}) collective-permute-start(bf16[400,384]{1,0:T(8,128)(2,1)S(1)} %get-tuple-element.107.refs_0_), channel_id=1, source_target_pairs={{0,8},{4,12},{8,0},{12,4},{16,24},{20,28},{24,16},{28,20},{1,9},{5... | collective-permute-start | bytes 921608 | tf_op jit(solution)/shard_map/ppermute | solution.py:460
  41.3 31.2 %collective-permute-start.7 = (bf16[384,896]{1,0:T(8,128)(2,1)S(1)}, bf16[384,896]{1,0:T(8,128)(2,1)S(1)}, u32[]{:S(2)}, u32[]{:S(2)}) collective-permute-start(bf16[384,896]{1,0:T(8,128)(2,1)S(1)} %bitcast.24), channel_id=1, source_target_pairs={{0,1},{1,0},{2,3},{3,2},{4,5},{5,4},{6,7},{7,6},{8,9},{9,8},{10,11... | collective-permute-start | bytes 2064392 | tf_op jit(solution)/shard_map/ppermute | solution.py:460
  46.9 17.8 %collective-permute-start.21 = (bf16[400,384]{1,0:T(8,128)(2,1)S(1)}, bf16[400,384]{1,0:T(8,128)(2,1)}, u32[]{:S(2)}, u32[]{:S(2)}) collective-permute-start(bf16[400,384]{1,0:T(8,128)(2,1)S(1)} %collective-permute-done.20.refs_4_), channel_id=1, source_target_pairs={{0,4},{4,0},{8,12},{12,8},{16,20},{20,16},{24,28},{28,24},{1,5},{5... | collective-permute-start | bytes 921608 | tf_op jit(solution)/shard_map/ppermute | solution.py:460
  48.5 22.4 %collective-permute-start.19 = (bf16[400,384]{1,0:T(8,128)(2,1)}, bf16[400,384]{1,0:T(8,128)(2,1)}, u32[]{:S(2)}, u32[]{:S(2)}) collective-permute-start(bf16[400,384]{1,0:T(8,128)(2,1)} %collective-permute-done.18.refs_2_), channel_id=1, source_target_pairs={{0,4},{4,0},{8,12},{12,8},{16,20},{20,16},{24,28},{28,24},{1,5},{5... | collective-permute-start | bytes 921608 | tf_op jit(solution)/shard_map/ppermute | solution.py:460
  86.2 32.1 %collective-permute-start.14 = (bf16[256,384]{1,0:T(8,128)(2,1)S(1)}, bf16[256,384]{1,0:T(8,128)(2,1)S(1)}, u32[]{:S(2)}, u32[]{:S(2)}) collective-permute-start(bf16[256,384]{1,0:T(8,128)(2,1)S(1)} %get-tuple-element.104), channel_id=1, source_target_pairs={{0,1},{1,0},{2,3},{3,2},{4,5},{5,4},{6,7},{7,6},{8,9},{9,8},{10,11... | collective-permute-start | bytes 589832 | tf_op jit(solution)/shard_map/ppermute | solution.py:460
  86.2 32.2 %collective-permute-start.15 = (bf16[256,384]{1,0:T(8,128)(2,1)S(1)}, bf16[256,384]{1,0:T(8,128)(2,1)S(1)}, u32[]{:S(2)}, u32[]{:S(2)}) collective-permute-start(bf16[256,384]{1,0:T(8,128)(2,1)S(1)} %get-tuple-element.105), channel_id=1, source_target_pairs={{0,2},{1,3},{2,0},{3,1},{4,6},{5,7},{6,4},{7,5},{8,10},{9,11},{10,... | collective-permute-start | bytes 589832 | tf_op jit(solution)/shard_map/ppermute | solution.py:460
  109.4 30.2 %collective-permute-start.24 = (bf16[256,384]{1,0:T(8,128)(2,1)S(1)}, bf16[256,384]{1,0:T(8,128)(2,1)S(1)}, u32[]{:S(2)}, u32[]{:S(2)}) collective-permute-start(bf16[256,384]{1,0:T(8,128)(2,1)S(1)} %get-tuple-element.126), channel_id=1, source_target_pairs={{0,1},{1,0},{2,3},{3,2},{4,5},{5,4},{6,7},{7,6},{8,9},{9,8},{10,11... | collective-permute-start | bytes 589832 | tf_op jit(solution)/shard_map/ppermute | solution.py:460
  110.0 29.5 %collective-permute-start.25 = (bf16[256,384]{1,0:T(8,128)(2,1)S(1)}, bf16[256,384]{1,0:T(8,128)(2,1)S(1)}, u32[]{:S(2)}, u32[]{:S(2)}) collective-permute-start(bf16[256,384]{1,0:T(8,128)(2,1)S(1)} %get-tuple-element.127), channel_id=1, source_target_pairs={{0,2},{1,3},{2,0},{3,1},{4,6},{5,7},{6,4},{7,5},{8,10},{9,11},{10,... | collective-permute-start | bytes 589832 | tf_op jit(solution)/shard_map/ppermute | solution.py:460
  118.3 21.9 %collective-permute-start.26 = (bf16[256,384]{1,0:T(8,128)(2,1)S(1)}, bf16[256,384]{1,0:T(8,128)(2,1)S(1)}, u32[]{:S(2)}, u32[]{:S(2)}) collective-permute-start(bf16[256,384]{1,0:T(8,128)(2,1)S(1)} %get-tuple-element.128), channel_id=1, source_target_pairs={{0,3},{1,2},{2,1},{3,0},{4,7},{5,6},{6,5},{7,4},{8,11},{9,10},{10,... | collective-permute-start | bytes 589832 | tf_op jit(solution)/shard_map/ppermute | solution.py:460
  118.4 31.0 %collective-permute-start.27 = (bf16[256,384]{1,0:T(8,128)(2,1)S(1)}, bf16[256,384]{1,0:T(8,128)(2,1)S(1)}, u32[]{:S(2)}, u32[]{:S(2)}) collective-permute-start(bf16[256,384]{1,0:T(8,128)(2,1)S(1)} %get-tuple-element.136), channel_id=1, source_target_pairs={{0,1},{1,0},{2,3},{3,2},{4,5},{5,4},{6,7},{7,6},{8,9},{9,8},{10,11... | collective-permute-start | bytes 589832 | tf_op jit(solution)/shard_map/ppermute | solution.py:460
  119.0 30.4 %collective-permute-start.28 = (bf16[256,384]{1,0:T(8,128)(2,1)S(1)}, bf16[256,384]{1,0:T(8,128)(2,1)S(1)}, u32[]{:S(2)}, u32[]{:S(2)}) collective-permute-start(bf16[256,384]{1,0:T(8,128)(2,1)S(1)} %get-tuple-element.137), channel_id=1, source_target_pairs={{0,2},{1,3},{2,0},{3,1},{4,6},{5,7},{6,4},{7,5},{8,10},{9,11},{10,... | collective-permute-start | bytes 589832 | tf_op jit(solution)/shard_map/ppermute | solution.py:460
  139.6 18.7 %collective-permute-start.30 = (bf16[256,384]{1,0:T(8,128)(2,1)S(1)}, bf16[256,384]{1,0:T(8,128)(2,1)S(1)}, u32[]{:S(2)}, u32[]{:S(2)}) collective-permute-start(bf16[256,384]{1,0:T(8,128)(2,1)S(1)} %get-tuple-element.147), channel_id=1, source_target_pairs={{0,1},{1,0},{2,3},{3,2},{4,5},{5,4},{6,7},{7,6},{8,9},{9,8},{10,11... | collective-permute-start | bytes 589832 | tf_op jit(solution)/shard_map/ppermute | solution.py:460
  140.2 18.1 %collective-permute-start.31 = (bf16[256,384]{1,0:T(8,128)(2,1)S(1)}, bf16[256,384]{1,0:T(8,128)(2,1)S(1)}, u32[]{:S(2)}, u32[]{:S(2)}) collective-permute-start(bf16[256,384]{1,0:T(8,128)(2,1)S(1)} %get-tuple-element.148), channel_id=1, source_target_pairs={{0,2},{1,3},{2,0},{3,1},{4,6},{5,7},{6,4},{7,5},{8,10},{9,11},{10,... | collective-permute-start | bytes 589832 | tf_op jit(solution)/shard_map/ppermute | solution.py:460
  168.5 16.5 %collective-permute-start.44 = (bf16[4,192,384]{2,1,0:T(8,128)(2,1)}, bf16[4,192,384]{2,1,0:T(8,128)(2,1)}, u32[]{:S(2)}, u32[]{:S(2)}) collective-permute-start(bf16[4,192,384]{2,1,0:T(8,128)(2,1)} %get-tuple-element.173), channel_id=1, source_target_pairs={{0,4},{4,0},{8,12},{12,8},{16,20},{20,16},{24,28},{28,24},{1,5},{5... | collective-permute-start | bytes 1769480 | tf_op jit(solution)/shard_map/ppermute | solution.py:460
  169.4 30.2 %collective-permute-start.40 = (bf16[4,56,1536]{2,1,0:T(8,128)(2,1)S(1)}, bf16[4,56,1536]{2,1,0:T(8,128)(2,1)S(1)}, u32[]{:S(2)}, u32[]{:S(2)}) collective-permute-start(bf16[4,56,1536]{2,1,0:T(8,128)(2,1)S(1)} %get-tuple-element.167), channel_id=1, source_target_pairs={{0,4},{4,0},{8,12},{12,8},{16,20},{20,16},{24,28},{28,24},{1,5},{5... | collective-permute-start | bytes 2064392 | tf_op jit(solution)/shard_map/ppermute | solution.py:460
  174.6 31.4 %collective-permute-start.34 = (bf16[4,48,896]{2,1,0:T(8,128)(2,1)S(1)}, bf16[4,48,896]{2,1,0:T(8,128)(2,1)S(1)}, u32[]{:S(2)}, u32[]{:S(2)}) collective-permute-start(bf16[4,48,896]{2,1,0:T(8,128)(2,1)S(1)} %get-tuple-element.158), channel_id=1, source_target_pairs={{0,4},{4,0},{8,12},{12,8},{16,20},{20,16},{24,28},{28,24},{1,5},{5... | collective-permute-start | bytes 1032200 | tf_op jit(solution)/shard_map/ppermute | solution.py:460
  187.9 16.4 %collective-permute-start.47 = (bf16[192,384]{1,0:T(8,128)(2,1)S(1)}, bf16[192,384]{1,0:T(8,128)(2,1)S(1)}, u32[]{:S(2)}, u32[]{:S(2)}) collective-permute-start(bf16[192,384]{1,0:T(8,128)(2,1)S(1)} %get-tuple-element.177), channel_id=1, source_target_pairs={{0,8},{4,12},{8,0},{12,4},{16,24},{20,28},{24,16},{28,20},{1,9},{5... | collective-permute-start | bytes 442376 | tf_op jit(solution)/shard_map/ppermute | solution.py:460
  201.4 19.5 %collective-permute-start.42 = (bf16[56,1536]{1,0:T(8,128)(2,1)S(1)}, bf16[56,1536]{1,0:T(8,128)(2,1)S(1)}, u32[]{:S(2)}, u32[]{:S(2)}) collective-permute-start(bf16[56,1536]{1,0:T(8,128)(2,1)S(1)} %get-tuple-element.170), channel_id=1, source_target_pairs={{0,16},{4,20},{8,24},{12,28},{16,0},{20,4},{24,8},{28,12},{1,17},{... | collective-permute-start | bytes 516104 | tf_op jit(solution)/shard_map/ppermute | solution.py:460
  201.4 19.5 %collective-permute-start.43 = (bf16[56,1536]{1,0:T(8,128)(2,1)S(1)}, bf16[56,1536]{1,0:T(8,128)(2,1)S(1)}, u32[]{:S(2)}, u32[]{:S(2)}) collective-permute-start(bf16[56,1536]{1,0:T(8,128)(2,1)S(1)} %get-tuple-element.171), channel_id=1, source_target_pairs={{0,8},{4,12},{8,0},{12,4},{16,24},{20,28},{24,16},{28,20},{1,9},{5... | collective-permute-start | bytes 516104 | tf_op jit(solution)/shard_map/ppermute | solution.py:460
  (76 other events, 578.4 us)
